TPU v7x, 128 devices: a whole 4x4x4 slice. The times are simulated.
128 devices in a mesh: ctx: 64 (over x, y_lo, z, core), mp: 2 (over y_hi).
Axes of the slice: x: 4, y: 4 (y_hi: 2, y_lo: 2; y = y_hi * 2 + y_lo), z: 4, core: 2. Of those that a mesh axis runs over, the one named last changes fastest.
Arguments:
- inputs: bfloat16 [8192, 2560], P('ctx'), may hold values from -6 to 6
- attn_gain: bfloat16 [2560], P('ctx'), may hold values from 0.099609375 to 1.8984375
- query_weight: bfloat16 [2560, 2560], P('ctx', 'mp'), may hold values from -0.125 to 0.125
- keyval_weight: bfloat16 [2560, 512], P('ctx'), may hold values from -0.125 to 0.125
- out_weight: bfloat16 [2560, 2560], P('mp', 'ctx'), may hold values from -3 to 3
- ffn_gain: bfloat16 [2560], P('ctx'), may hold values from 0.099609375 to 1.8984375
- gate_weight: bfloat16 [2560, 7680], P('ctx', 'mp'), may hold values from -0.125 to 0.125
- up_weight: bfloat16 [2560, 7680], P('ctx', 'mp'), may hold values from -0.125 to 0.125
- down_weight: bfloat16 [7680, 2560], P('mp', 'ctx'), may hold values from -0.0625 to 0.0625
- positions: int32 [8192], replicated, may hold values from 0 to 10239, as said below
- cotangent: bfloat16 [8192, 2560], P('ctx'), may hold values from -6 to 6
Outputs:
- activations: bfloat16 [8192, 2560], P('ctx')
- input_grad: float32 [8192, 2560], P('ctx')
- attn_gain_grad: float32 [2560], P('ctx')
- query_weight_grad: float32 [2560, 2560], P('ctx', 'mp')
- keyval_weight_grad: float32 [2560, 512], P('ctx')
- out_weight_grad: float32 [2560, 2560], P('mp', 'ctx')
- ffn_gain_grad: float32 [2560], P('ctx')
- gate_weight_grad: float32 [2560, 7680], P('ctx', 'mp')
- up_weight_grad: float32 [2560, 7680], P('ctx', 'mp')
- down_weight_grad: float32 [7680, 2560], P('mp', 'ctx')
Inputs may be any that keep to these rules, and one draw needn't show every extreme that they name: positions strictly increase along the sequence.
All inputs are finite; a program needn't handle non-finite values.
Results may differ from a plain program's by a relative error of at most 0.017.
Values may be sent and summed in bfloat16 or wider, within the bound.
No kernel may reach another device: no remote copies, remote signals or barrier semaphores. Data moves between devices by JAX's collectives and lax.ppermute only.
A program may use at most 320 MiB of HBM per device.

v0:
```python
import functools

import jax
import jax.numpy as jnp
from jax import lax
from jax.experimental import pallas as pl
from jax.experimental.pallas import tpu as pltpu
from jax.sharding import Mesh, PartitionSpec as P

HD = 256
WINDOW = 2048
EPS = 1e-06

PLANES = 4
RANK_SIZES = (2, 4, 2)
RANKS = 16
CHIPS = 8
X = "x"
R = ("yl", "z", "c")
CHIP = ("yl", "z")
CORE = "c"
M = "mp"

F32 = jnp.float32
BF16 = jnp.bfloat16


def after(value, *earlier):
    return lax.optimization_barrier((value,) + earlier)[0]


def rms_scale(values):
    return lax.rsqrt(jnp.mean(values * values, axis=-1, keepdims=True) + EPS)


def norm_back(values, scale_rows, weighted):
    return scale_rows * weighted - values * scale_rows**3 * jnp.mean(
        weighted * values, axis=-1, keepdims=True
    )


def to_plane(block, shift):
    return lax.ppermute(block, X, [(i, (i + shift) % PLANES) for i in range(PLANES)])


def swap(block):
    return lax.ppermute(block, M, [(0, 1), (1, 0)])


def swap_cores(block):
    return lax.ppermute(block, CORE, [(0, 1), (1, 0)])


def rounded(values):
    return lax.reduce_precision(values, 8, 7).astype(BF16)


def sum_mp(part):
    low = rounded(part)
    return low.astype(F32) + swap(low).astype(F32)


def gather_planes(block):
    half = block.shape[0] // 2
    after = to_plane(block, -1)
    before = to_plane(block, 1)
    far_top = to_plane(before[:half], 1)
    far_low = to_plane(after[half:], -1)
    return jnp.concatenate([block, after, far_top, far_low, before], 0)


def collect_planes(block):
    return [block, to_plane(block, 3), to_plane(block, 2), to_plane(block, 1)]


def reduce_far(part):
    rows = part.shape[0] // PLANES
    half = rows // 2
    own, after_one, far, before_one = (
        part[i * rows : (i + 1) * rows].astype(F32) for i in range(PLANES)
    )
    far = rounded(far)
    top = to_plane(far[:half], 1).astype(F32)
    low = to_plane(far[half:], -1).astype(F32)
    after_one = jnp.concatenate([after_one[:half] + top, after_one[half:]], 0)
    before_one = jnp.concatenate([before_one[:half], before_one[half:] + low], 0)
    return own, rounded(after_one), rounded(before_one)


def reduce_near(own, after_one, before_one):
    return own + to_plane(before_one, -1).astype(F32) + to_plane(after_one, 1).astype(F32)


def reduce_planes(part):
    return reduce_near(*reduce_far(part))


def pick(blocks, index):
    return lax.dynamic_index_in_dim(blocks, lax.rem(index + PLANES, PLANES), 0, keepdims=False)


def natural(blocks):
    plane = lax.axis_index(X)
    return [pick(blocks, p - plane) for p in range(PLANES)]


def send_planes(blocks):
    plane = lax.axis_index(X)
    return [pick(blocks, plane)] + [
        to_plane(pick(blocks, plane + k), k) for k in range(1, PLANES)
    ]


def exchange_planes(blocks):
    plane = lax.axis_index(X)
    got = jnp.stack(send_planes(blocks))
    return [pick(got, plane - p) for p in range(PLANES)]


def cut_planes(values):
    rows, width = values.shape
    got = send_planes(values.reshape(rows, PLANES, width // PLANES).swapaxes(0, 1))
    return jnp.concatenate([got[0], got[3], got[2], got[1]], 0)


def cut_features(blocks):
    got = send_planes(blocks)
    return [got[0], got[3], got[2], got[1]]


def join_planes(blocks):
    got = jnp.stack([blocks[0]] + [to_plane(blocks[k], k) for k in range(1, PLANES)])
    plane = lax.axis_index(X)
    return jnp.concatenate([pick(got, plane - p) for p in range(PLANES)], 1)


def permute_features(values):
    rows, width = values.shape
    cut = values.reshape(rows, PLANES, RANKS, width // (PLANES * RANKS))
    return cut.swapaxes(1, 2).reshape(rows, width)


def restore_features(values):
    rows, width = values.shape
    cut = values.reshape(rows, RANKS, PLANES, width // (PLANES * RANKS))
    return cut.swapaxes(1, 2).reshape(rows, width)


def spread(block, axes, size):
    rows, columns = block.shape
    copies = jnp.broadcast_to(block[None], (size, rows, columns)).reshape(size * rows, columns)
    return lax.all_to_all(copies, axes, 0, 0, tiled=True)


def gather_rows(block):
    return lax.all_gather(block, R, axis=0, tiled=True)


def dot_rows(left, right):
    return lax.dot_general(left, right, (((1,), (1,)), ((), ())), preferred_element_type=F32)


def dot_tokens(left, right):
    return lax.dot_general(left, right, (((0,), (0,)), ((), ())), preferred_element_type=F32)


def softmax_parts(query, parts, biases):
    scale = HD ** (-0.5)
    scores = [dot_rows(query, part[0]) * scale + bias[...] for part, bias in zip(parts, biases)]
    top = functools.reduce(
        jnp.maximum, [jnp.max(score, axis=-1, keepdims=True) for score in scores]
    )
    scores = [jnp.exp(score - top) for score in scores]
    inverse = 1.0 / sum(jnp.sum(score, axis=-1, keepdims=True) for score in scores)
    return [score * inverse for score in scores]


def attend_kernel(count, query, *refs):
    parts, biases, out = refs[:count], refs[count : 2 * count], refs[2 * count]
    weights = softmax_parts(query[...], parts, biases)
    out[...] = sum(
        jnp.dot(weight.astype(BF16), part[1], preferred_element_type=F32)
        for weight, part in zip(weights, parts)
    ).astype(out.dtype)


def attend_back_kernel(
    core, query, out_grad, attended, token_scale, *refs
):
    parts, biases, refs = refs[:3], refs[3:6], refs[6:]
    both, window_grad, last_grad, refs = refs[0], refs[1], refs[2], refs[3:]
    queries, out_grads, refs = refs[0], refs[1], refs[2:]
    weights_all, scores_all = refs[:3], refs[3:]
    head = pl.program_id(0)
    heads = pl.num_programs(0)
    rows = query.shape[0]
    here = pl.ds(pl.multiple_of(head * rows, rows), rows)
    scale = HD ** (-0.5)
    weights = softmax_parts(query[...], parts, biases)
    grad = out_grad[...]
    probs = [dot_rows(grad, part[1]) for part in parts]
    inner = sum(
        jnp.sum(weight * prob, axis=-1, keepdims=True) for weight, prob in zip(weights, probs)
    )
    scores = [
        (weight * (prob - inner)).astype(BF16) for weight, prob in zip(weights, probs)
    ]
    both[:, pl.ds(pl.multiple_of(head * HD, HD), HD)] = (
        sum(
            jnp.dot(score, part[0], preferred_element_type=F32)
            for score, part in zip(scores, parts)
        )
        * (token_scale[...] * scale)
    ).astype(both.dtype)
    both[:, pl.ds(pl.multiple_of((heads + head) * HD, HD), HD)] = attended[...]
    queries[here, :] = query[...]
    out_grads[here, :] = grad
    for i in range(3):
        weights_all[i][here, :] = weights[i].astype(BF16)
        scores_all[i][here, :] = scores[i]

    @pl.when(head == heads - 1)
    def _():
        for i in range(3):
            key = (dot_tokens(scores_all[i][...], queries[...]) * scale).astype(BF16)
            value = dot_tokens(weights_all[i][...], out_grads[...]).astype(BF16)
            if i == 2:
                last_grad[0] = key
                last_grad[1] = value
            else:
                which = core[0] if i == 0 else 1 - core[0]
                shape = (CHIPS, 1, rows, HD)
                window_grad[0, :, pl.ds(which, 1)] = key.reshape(shape)
                window_grad[1, :, pl.ds(which, 1)] = value.reshape(shape)


def whole_spec(shape):
    return pl.BlockSpec(shape, lambda i: (0,) * len(shape))


def attend(queries, parts, biases):
    rows, width = queries.shape
    span = sum(bias.shape[1] for bias in biases)
    head_spec = pl.BlockSpec((rows, HD), lambda i: (0, i))
    return pl.pallas_call(
        functools.partial(attend_kernel, len(parts)),
        grid=(width // HD,),
        in_specs=[head_spec] + [whole_spec(v.shape) for v in (*parts, *biases)],
        out_specs=head_spec,
        out_shape=jax.ShapeDtypeStruct(queries.shape, BF16),
        compiler_params=pltpu.CompilerParams(vmem_limit_bytes=48 * 1024 * 1024),
        cost_estimate=pl.CostEstimate(
            flops=4 * rows * width * span,
            bytes_accessed=4 * span * HD + 4 * rows * span + 4 * queries.size,
            transcendentals=rows * span * (width // HD),
        ),
    )(queries, *parts, *biases)


def attend_back(core, queries, out_grad, attended, token_scale, parts, biases):
    rows, width = queries.shape
    heads = width // HD
    spans = [bias.shape[1] for bias in biases]
    head_spec = pl.BlockSpec((rows, HD), lambda i: (0, i))
    shapes = [(rows, 2 * width), (2, CHIPS, 2, rows, HD), parts[-1].shape]
    return pl.pallas_call(
        attend_back_kernel,
        grid=(heads,),
        in_specs=[pl.BlockSpec(memory_space=pltpu.SMEM), head_spec, head_spec, head_spec]
        + [whole_spec(v.shape) for v in (token_scale, *parts, *biases)],
        out_specs=[whole_spec(shape) for shape in shapes],
        out_shape=[jax.ShapeDtypeStruct(shape, BF16) for shape in shapes],
        scratch_shapes=[pltpu.VMEM((heads * rows, HD), BF16)] * 2
        + [pltpu.VMEM((heads * rows, span), BF16) for span in spans] * 2,
        compiler_params=pltpu.CompilerParams(vmem_limit_bytes=56 * 1024 * 1024),
        cost_estimate=pl.CostEstimate(
            flops=10 * rows * width * sum(spans),
            bytes_accessed=8 * sum(spans) * HD + 4 * rows * sum(spans) + 6 * queries.size,
            transcendentals=rows * sum(spans) * heads,
        ),
    )(core.reshape(1), queries, out_grad, attended, token_scale, *parts, *biases)


def geglu_kernel(tokens, cot, gate_weight, up_weight, down_weight, hidden, gate_up):
    step = pl.program_id(0)
    block = gate_weight.shape[1]
    gate = jnp.dot(tokens[...], gate_weight[...], preferred_element_type=F32)
    up = jnp.dot(tokens[...], up_weight[...], preferred_element_type=F32)
    hidden_grad = jnp.dot(cot[...], down_weight[...], preferred_element_type=F32)
    hidden_grad = hidden_grad.astype(BF16).astype(F32)
    root = 0.7978845608028654
    square = gate * gate
    bend = jnp.tanh(root * gate * (1.0 + 0.044715 * square))
    half = 0.5 * (1.0 + bend)
    gelu = gate * half
    slope = half + 0.5 * gate * (1.0 - bend * bend) * (root * (1.0 + 3 * 0.044715 * square))
    here = pl.ds(pl.multiple_of(step * block, block), block)
    hidden[:, here] = (gelu * up).astype(BF16)
    gate_up[:, here] = (hidden_grad * up * slope).astype(BF16)
    there = pl.ds(pl.multiple_of(hidden.shape[1] + step * block, block), block)
    gate_up[:, there] = (hidden_grad * gelu).astype(BF16)


def geglu(tokens, cot, weights):
    rows, width = tokens.shape
    units = weights.shape[1] // 3
    block = 256 if units % 256 == 0 else 128
    steps = units // block
    token_spec = pl.BlockSpec(tokens.shape, lambda i: (0, 0), pipeline_mode=pl.Buffered(1))
    return pl.pallas_call(
        geglu_kernel,
        grid=(steps,),
        in_specs=[
            token_spec,
            token_spec,
            pl.BlockSpec((width, block), lambda i: (0, i)),
            pl.BlockSpec((width, block), lambda i: (0, steps + i)),
            pl.BlockSpec((width, block), lambda i: (0, 2 * steps + i)),
        ],
        out_specs=[whole_spec((rows, units)), whole_spec((rows, 2 * units))],
        out_shape=[
            jax.ShapeDtypeStruct((rows, units), BF16),
            jax.ShapeDtypeStruct((rows, 2 * units), BF16),
        ],
        compiler_params=pltpu.CompilerParams(vmem_limit_bytes=56 * 1024 * 1024),
        cost_estimate=pl.CostEstimate(
            flops=2 * rows * width * 3 * units,
            bytes_accessed=2 * weights.size + 4 * tokens.size + 6 * rows * units,
            transcendentals=rows * units,
        ),
    )(tokens, cot, weights, weights, weights)


def outer_kernel(count, *refs):
    out = refs[-1]
    first = 0
    for i in range(count):
        left, right = refs[2 * i], refs[2 * i + 1]
        columns = right.shape[1]
        tokens_first = left.shape[0] == right.shape[0]
        step = 512 if columns % 512 == 0 else columns
        for at in range(0, columns, step):
            out[:, first + at : first + at + step] = lax.dot_general(
                left[...],
                right[:, at : at + step],
                (((0 if tokens_first else 1,), (0,)), ((), ())),
                preferred_element_type=F32,
            ).astype(out.dtype)
        first += columns


def token_outer(*pairs):
    tokens, height = pairs[0][0].shape
    columns = sum(right.shape[1] for _, right in pairs)
    block = next(size for size in (512, 640, 256, 128) if height % size == 0)
    specs, operands = [], []
    for left, right in pairs:
        specs += [
            pl.BlockSpec((tokens, block), lambda i: (0, i))
            if left.shape[0] == tokens
            else pl.BlockSpec((block, tokens), lambda i: (i, 0)),
            pl.BlockSpec(right.shape, lambda i: (0, 0)),
        ]
        operands += [left, right]
    return pl.pallas_call(
        functools.partial(outer_kernel, len(pairs)),
        grid=(height // block,),
        in_specs=specs,
        out_specs=pl.BlockSpec((block, columns), lambda i: (i, 0)),
        out_shape=jax.ShapeDtypeStruct((height, columns), BF16),
        compiler_params=pltpu.CompilerParams(vmem_limit_bytes=40 * 1024 * 1024),
        cost_estimate=pl.CostEstimate(
            flops=2 * tokens * height * columns,
            bytes_accessed=2 * height * columns + 2 * tokens * (height * len(pairs) + columns),
            transcendentals=0,
        ),
    )(*operands)


def attn_outer_kernel(*refs):
    inputs, cuts, boths = refs[0], refs[1:5], refs[5:9]
    out = refs[9]
    rows, width = boths[0].shape[0], boths[0].shape[1] // 2
    out[:, :width] = sum(
        dot_tokens(inputs[k * rows : (k + 1) * rows, :], boths[k][:, :width])
        for k in range(PLANES)
    ).astype(out.dtype)
    out[:, width:] = sum(
        jnp.dot(cuts[k][...], boths[k][:, width:], preferred_element_type=F32)
        for k in range(PLANES)
    ).astype(out.dtype)


def attn_outer(inputs, cuts, boths):
    height, columns = inputs.shape[1], boths[0].shape[1]
    rows = boths[0].shape[0]
    block = 128
    return pl.pallas_call(
        attn_outer_kernel,
        grid=(height // block,),
        in_specs=[pl.BlockSpec((inputs.shape[0], block), lambda i: (0, i))]
        + [pl.BlockSpec((block, rows), lambda i: (i, 0))] * PLANES
        + [whole_spec(boths[0].shape)] * PLANES,
        out_specs=pl.BlockSpec((block, columns), lambda i: (i, 0)),
        out_shape=jax.ShapeDtypeStruct((height, columns), BF16),
        compiler_params=pltpu.CompilerParams(vmem_limit_bytes=40 * 1024 * 1024),
        cost_estimate=pl.CostEstimate(
            flops=2 * PLANES * rows * height * columns,
            bytes_accessed=2 * (height + PLANES * rows) * columns + 4 * inputs.size,
            transcendentals=0,
        ),
    )(inputs, *cuts, *boths)


def input_back_kernel(*refs):
    boths, keyvals, query_rows, keyval_rows = refs[:4], refs[4:8], refs[8], refs[9]
    keyval_out, outs = refs[10], refs[11:]
    rows, width = boths[0].shape[0], boths[0].shape[1] // 2
    for k in range(PLANES):
        keyval = (
            keyvals[k][:rows].astype(F32) + keyvals[(k + 1) % PLANES][rows:].astype(F32)
        ).astype(BF16)
        keyval_out[k * rows : (k + 1) * rows] = keyval
        outs[k][...] = (
            dot_rows(boths[k][:, :width], query_rows[...]) + dot_rows(keyval, keyval_rows[...])
        ).astype(outs[k].dtype)


def input_back(boths, keyvals, query_rows, keyval_rows):
    rows = boths[0].shape[0]
    height = query_rows.shape[0]
    shapes = [(PLANES * rows, HD)] + [(rows, height)] * PLANES
    operands = (*boths, *keyvals, query_rows, keyval_rows)
    return pl.pallas_call(
        input_back_kernel,
        grid=(1,),
        in_specs=[whole_spec(v.shape) for v in operands],
        out_specs=[whole_spec(shape) for shape in shapes],
        out_shape=[jax.ShapeDtypeStruct(shape, BF16) for shape in shapes],
        compiler_params=pltpu.CompilerParams(vmem_limit_bytes=40 * 1024 * 1024),
        cost_estimate=pl.CostEstimate(
            flops=2 * PLANES * rows * height * query_rows.shape[1],
            bytes_accessed=2 * sum(v.size for v in operands) + 2 * PLANES * rows * height,
            transcendentals=0,
        ),
    )(*operands)


def join_kernel(padded, gate_weight, up_weight, gain, *refs):
    pieces, outs, gain_out = refs[:PLANES], refs[PLANES : PLANES + 3], refs[PLANES + 3]
    units = gate_weight.shape[1] // PLANES
    total = jnp.zeros((gate_weight.shape[0], 1), F32)
    for p in range(PLANES):
        columns = slice(p * units, (p + 1) * units)
        gate = pieces[p][:, :units].astype(F32)
        up = pieces[p][:, padded : padded + units].astype(F32)
        total += jnp.sum(
            gate_weight[:, columns].astype(F32) * gate + up_weight[:, columns].astype(F32) * up,
            axis=1,
            keepdims=True,
        )
        outs[0][:, columns] = gate * gain[...]
        outs[1][:, columns] = up * gain[...]
        outs[2][:, columns] = pieces[p][:, 2 * padded : 2 * padded + units].astype(F32)
    gain_out[...] = total


def join(pieces, gate_weight, up_weight, gain):
    shape = gate_weight.shape
    padded = pieces[0].shape[1] // 3
    operands = (gate_weight, up_weight, gain, *pieces)
    shapes = [shape] * 3 + [(shape[0], 1)]
    return pl.pallas_call(
        functools.partial(join_kernel, padded),
        grid=(1,),
        in_specs=[whole_spec(v.shape) for v in operands],
        out_specs=[whole_spec(one) for one in shapes],
        out_shape=[jax.ShapeDtypeStruct(one, F32) for one in shapes],
        compiler_params=pltpu.CompilerParams(vmem_limit_bytes=40 * 1024 * 1024),
        cost_estimate=pl.CostEstimate(
            flops=10 * gate_weight.size,
            bytes_accessed=24 * gate_weight.size,
            transcendentals=0,
        ),
    )(*operands)


def body(
    inputs,
    attn_gain,
    query_weight,
    keyval_weight,
    out_weight,
    ffn_gain,
    gate_weight,
    up_weight,
    down_weight,
    positions,
    cotangent,
):
    rows, width = inputs.shape
    own = attn_gain.shape[0]
    query_width = query_weight.shape[1]
    head_count = query_width // HD
    units = gate_weight.shape[1] // PLANES
    padded = -(-units // 128) * 128
    scale = HD ** (-0.5)
    plane = lax.axis_index(X)
    rank = lax.axis_index(R)
    half = lax.axis_index(M)
    core = lax.axis_index(CORE)
    chip = lax.axis_index(CHIP)
    chips = jnp.arange(CHIPS, dtype=jnp.int32)
    ahead = (chips >= chip)[:, None, None]
    at_home = (chips == chip)[:, None, None]
    gain_one = attn_gain.astype(F32)[:, None]
    gain_two = ffn_gain.astype(F32)[:, None]

    keyval_own = (
        lax.dynamic_slice_in_dim(keyval_weight, half * HD, HD, 1).astype(F32) * gain_one
    ).astype(BF16)
    query_own = (query_weight.astype(F32) * gain_one).astype(BF16)
    inputs_cut = cut_planes(inputs)
    tokens_in = inputs.astype(F32)
    scale_attn = rms_scale(tokens_in)
    scale_before = to_plane(scale_attn.reshape(1, rows), 1).reshape(rows, 1)

    def cut(weight):
        blocks = weight.reshape(own, PLANES, units)
        return jnp.pad(blocks, ((0, 0), (0, 0), (0, padded - units))).swapaxes(0, 1)

    ffn_own = jnp.concatenate(
        [
            cut((gate_weight.astype(F32) * gain_two).astype(BF16)),
            cut((up_weight.astype(F32) * gain_two).astype(BF16)),
            cut(down_weight.T),
        ],
        2,
    ).reshape(PLANES * own, 3 * padded)
    out_planes = lax.all_gather(out_weight.T, X, axis=0, tiled=True)
    both = gather_rows(jnp.concatenate([query_own, out_planes], 0))
    ffn_own = lax.all_to_all(after(ffn_own, out_planes), X, 0, 0, tiled=True)
    ffn = gather_rows(ffn_own)
    keyval_rows = spread(after(keyval_own, ffn_own), R, RANKS)

    ranks = jnp.arange(RANKS, dtype=jnp.int32)
    block_own = plane * RANKS + rank
    offsets = jnp.arange(rows, dtype=jnp.int32)
    span = RANKS * rows
    pos_own = lax.dynamic_slice_in_dim(positions, plane * span, span, 0).reshape(RANKS, rows)
    pos_before = lax.dynamic_slice_in_dim(
        positions, jnp.maximum(plane - 1, 0) * span, span, 0
    ).reshape(RANKS, rows)
    pos_last = lax.dynamic_slice_in_dim(pos_before, rank, 1, 0)
    def in_parts(own_values, before_values, last_values):
        chosen = jnp.where((ranks <= rank)[:, None], own_values, before_values)
        cores = chosen.reshape(CHIPS, 2, rows)
        parts = [
            lax.dynamic_index_in_dim(cores, index, 1, keepdims=False).reshape(-1)
            for index in (core, 1 - core)
        ]
        return jnp.concatenate(parts + [last_values.reshape(-1)])

    index_own = ((plane * RANKS + ranks) * rows)[:, None] + offsets[None]
    key_index = in_parts(
        index_own, index_own - span, (block_own - RANKS) * rows + offsets
    )
    pos_keys = in_parts(pos_own, pos_before, pos_last)
    pos_query = lax.dynamic_slice_in_dim(positions, block_own * rows, rows, 0)
    query_index = block_own * rows + offsets
    allowed = (
        (key_index[None, :] >= 0)
        & (key_index[None, :] <= query_index[:, None])
        & (pos_query[:, None] - pos_keys[None, :] < WINDOW)
    )

    bias = jnp.where(allowed, 0.0, -1e30)
    part_span = CHIPS * rows
    biases = [
        bias[:, :part_span],
        bias[:, part_span : 2 * part_span],
        bias[:, 2 * part_span :],
    ]
    residual, cot = lax.optimization_barrier(
        (
            permute_features(after(inputs, ffn_own)),
            permute_features(after(cotangent, ffn_own)),
        )
    )

    keyval = (
        reduce_planes(
            jnp.dot(
                after(inputs_cut, residual, cot),
                keyval_rows,
                preferred_element_type=F32,
            )
        )
        * scale_attn
    ).astype(BF16)
    keyval_before = to_plane(keyval, 1)
    before_other = to_plane(swap(keyval), 1)
    down = ffn[:, 2 * padded :]

    both = both.reshape(RANKS, (1 + PLANES) * own, query_width)
    query_rows = lax.optimization_barrier(both[:, :own].reshape(RANKS * own, query_width))
    out_rows = both[:, own:].reshape(width, query_width)
    queries_part = jnp.dot(after(inputs_cut, before_other), query_rows, preferred_element_type=F32)
    queries_sum = reduce_planes(queries_part)
    first = half == 0
    last = jnp.where(
        first,
        jnp.stack([keyval_before, before_other]),
        jnp.stack([before_other, keyval_before]),
    )
    chosen = jnp.where(ahead, keyval[None], keyval_before[None])
    sent = jnp.broadcast_to(chosen[None], (2, CHIPS, rows, HD))
    met = lax.all_to_all(
        sent.reshape(2 * CHIPS * rows, HD), (M,) + CHIP, 0, 0, tiled=True
    ).reshape(2, CHIPS, rows, HD)
    met_lent = jnp.where(at_home & (core == 1), last[:, None], met)
    met_other = swap_cores(after(met_lent, queries_sum))
    window = [v.reshape(2, CHIPS * rows, HD) for v in (met, met_other)]
    queries, out_rows = lax.optimization_barrier(
        ((queries_sum * scale_attn).astype(BF16), out_rows)
    )

    attended = attend(queries, window + [last], biases)
    branch_part = jnp.einsum("te,de->td", attended, out_rows, preferred_element_type=F32)
    branch = sum_mp(branch_part)
    cot_all = gather_planes(after(cot, queries))
    middle = residual.astype(F32) + after(branch, cot_all)

    scale_ffn = rms_scale(middle)
    normed = (middle * scale_ffn).astype(BF16)
    normed_all = gather_planes(normed)
    hidden, gate_up_low = geglu(normed_all, cot_all, ffn)
    ffn_grad_part = token_outer((normed_all, gate_up_low), (cot_all, hidden))
    ffn_grad_rows = lax.psum_scatter(ffn_grad_part, R, scatter_dimension=0, tiled=True)
    gate_up_low = after(gate_up_low, ffn_grad_part)
    weighted_part = jnp.einsum(
        "tf,ef->te", gate_up_low, ffn[:, : 2 * padded], preferred_element_type=F32
    ).astype(BF16)
    weighted_low = rounded(reduce_planes(weighted_part))
    weighted = weighted_low.astype(F32) + swap(weighted_low).astype(F32)

    middle_grad = cot.astype(F32) + norm_back(middle, scale_ffn, weighted)
    branch_low = middle_grad.astype(BF16)
    attended_grad = jnp.dot(branch_low, out_rows, preferred_element_type=F32).astype(BF16)
    query_both, window_grad, last_grad = attend_back(
        core, queries, attended_grad, attended, scale_attn, window + [last], biases
    )
    gathered = collect_planes(query_both)
    branch_late = after(branch_low, *gathered)
    branch_turned = branch_late.T.reshape(RANKS, PLANES, own, rows)
    branch_cut = cut_features(branch_turned.swapaxes(0, 1).reshape(PLANES, RANKS * own, rows))

    ffn_part = jnp.einsum(
        "tf,ef->te", after(hidden, *branch_cut), down, preferred_element_type=F32
    )
    ffn_low = rounded(reduce_planes(ffn_part))

    returned = lax.all_to_all(
        window_grad.reshape(2 * RANKS * rows, HD), (M,) + R, 0, 0, tiled=True
    ).reshape(2, RANKS, rows, HD)
    last_other = swap(jnp.where(first, last_grad[1], last_grad[0]))
    last_mine = jnp.where(first, last_grad[0], last_grad[1])
    own_plane = (ranks >= rank)[:, None, None]
    own_sum = jnp.sum(jnp.where(own_plane, returned, 0).astype(F32), (0, 1))
    before_sum = (
        jnp.sum(jnp.where(own_plane, 0, returned).astype(F32), (0, 1))
        + last_mine.astype(F32)
        + last_other.astype(F32)
    )

    keyval_pieces = collect_planes(
        rounded(jnp.concatenate([own_sum * scale_attn, before_sum * scale_before], 0))
    )
    attn_grad_part = attn_outer(inputs_cut, branch_cut, gathered)
    attn_width = attn_grad_part.shape[1]
    attn_cores = attn_grad_part.reshape(CHIPS, 2, own, attn_width)
    attn_lent = swap_cores(lax.dynamic_index_in_dim(attn_cores, 1 - core, 1, keepdims=False))
    attn_kept = lax.dynamic_index_in_dim(attn_cores, core, 1, keepdims=False)
    attn_chip = rounded(attn_kept.astype(F32) + attn_lent.astype(F32))
    attn_met = lax.all_to_all(
        attn_chip.reshape(CHIPS * own, attn_width), CHIP, 0, 0, tiled=True
    )
    keyval_all, *input_parts = input_back(gathered, keyval_pieces, query_rows, keyval_rows)
    ffn_grad_rows, middle_late, ffn_low, attn_met = lax.optimization_barrier(
        (ffn_grad_rows, middle_grad, ffn_low, attn_met)
    )
    input_parts[1] = after(input_parts[1], attn_met)
    weighted_low = rounded(join_planes(input_parts).astype(F32))
    weighted_other = swap(weighted_low)
    ffn_grad_rows = after(ffn_grad_rows, weighted_low)
    attn_base = jnp.sum(attn_met.reshape(CHIPS, own, attn_width).astype(F32), 0)
    query_base = attn_base[:, :query_width]
    out_weight_grad = attn_base[:, query_width : 2 * query_width].T
    keyval_met = lax.all_to_all(
        after(token_outer((inputs_cut, keyval_all)), attn_met), R, 0, 0, tiled=True
    )
    keyval_mine = jnp.sum(keyval_met.reshape(RANKS, own, HD).astype(F32), 0)
    keyval_other = swap(after(keyval_mine, weighted_other))
    keyval_base = jnp.concatenate(
        [
            jnp.where(first, keyval_mine, keyval_other),
            jnp.where(first, keyval_other, keyval_mine),
        ],
        1,
    )

    weighted_one = weighted_low.astype(F32) + weighted_other.astype(F32)
    input_grad = (
        restore_features(middle_late)
        + weighted_one
        - tokens_in
        * scale_attn**2
        * jnp.mean(weighted_one * tokens_in, axis=-1, keepdims=True)
    )

    ffn_sum = ffn_low.astype(F32) + swap(ffn_low).astype(F32)
    activations = restore_features((middle + ffn_sum).astype(BF16))
    ffn_grad_own = exchange_planes(ffn_grad_rows.reshape(PLANES, own, 3 * padded))
    gate_weight_grad, up_weight_grad, down_rows, ffn_gain_part = join(
        ffn_grad_own, gate_weight, up_weight, gain_two
    )

    gain_parts = jnp.stack(
        [jnp.sum(query_weight.astype(F32) * query_base, axis=1), ffn_gain_part[:, 0]]
    )
    gain_sums = gain_parts + swap(after(gain_parts, weighted_other))
    ffn_gain_grad = gain_sums[1]
    attn_gain_grad = gain_sums[0] + jnp.sum(keyval_weight.astype(F32) * keyval_base, axis=1)

    return (
        activations,
        input_grad,
        attn_gain_grad,
        query_base * gain_one,
        keyval_base * gain_one,
        out_weight_grad,
        ffn_gain_grad,
        gate_weight_grad,
        up_weight_grad,
        down_rows.T,
    )


def solution(mesh):
    axes = (X,) + R
    cut = Mesh(mesh.devices.reshape((PLANES,) + RANK_SIZES + (2,)), axes + (M,))
    return jax.shard_map(
        body,
        mesh=cut,
        in_specs=(
            P(axes, None),
            P(axes),
            P(axes, M),
            P(axes, None),
            P(M, axes),
            P(axes),
            P(axes, M),
            P(axes, M),
            P(M, axes),
            P(),
            P(axes, None),
        ),
        out_specs=(
            P(axes, None),
            P(axes, None),
            P(axes),
            P(axes, M),
            P(axes, None),
            P(M, axes),
            P(axes),
            P(axes, M),
            P(axes, M),
            P(M, axes),
        ),
        check_vma=False,
    )
```

profile of v0, /device:TPU:0, one launch (start us, length us, event | category | flops | bytes accessed | tf_op | source)
XLA Modules:
  0.0 474.3 jit_solution(15292568841539230272)
XLA Ops:
  7.3 13.3 %all_gather.9 = bf16[160,1280]{1,0:T(8,128)(2,1)S(1)} all-gather(bf16[40,1280]{1,0:T(8,128)(2,1)} %bitcast.187), channel_id=1, replica_groups=mesh['x'=4,'yl'=2,'z'=4,'c'=2,'mp'=2] {'x'}, dimensions={0}, use_global_device_ids=true | all-gather | bytes 512000 | tf_op jit(solution)/shard_map/all_gather | solution.py:540
  26.2 16.2 %all_to_all.56 = bf16[4,40,3072]{2,1,0:T(8,128)(2,1)} all-to-all(bf16[4,40,3072]{2,1,0:T(8,128)(2,1)S(1)} %copy.55), channel_id=1, replica_groups=mesh['x'=4,'yl'=2,'z'=4,'c'=2,'mp'=2] {'x'}, dimensions={0} | all-to-all | bytes 1966080 | tf_op jit(solution)/shard_map/all_to_all | solution.py:542
  48.7 6.4 %all-to-all-start.1 = ((bf16[16,40,256]{2,1,0:T(8,128)(2,1)}), bf16[16,40,256]{2,1,0:T(8,128)(2,1)S(1)}, u32[]{:S(2)}, u32[]{:S(2)}) async-start(bf16[16,40,256]{2,1,0:T(8,128)(2,1)} %broadcast_in_dim.118), calls=%async_computation.1 | async-start | bytes 655360 | tf_op jit(solution)/shard_map/all_to_all | solution.py:152
  57.9 9.8 %all-to-all-done.1 = bf16[16,40,256]{2,1,0:T(8,128)(2,1)S(1)} async-done(((bf16[16,40,256]{2,1,0:T(8,128)(2,1)}), bf16[16,40,256]{2,1,0:T(8,128)(2,1)S(1)}, u32[]{:S(2)}, u32[]{:S(2)}) %all-to-all-start.1) | async-done | bytes 327712 | tf_op jit(solution)/shard_map/all_to_all | solution.py:152
  68.1 3.3 collective-permute-start.3
  73.0 3.5 collective-permute-done.5
  82.3 3.0 collective-permute-start.7
  89.3 4.4 collective-permute-done.8
  96.7 3.2 collective-permute-start.9
  101.0 4.3 all-to-all-start.2
  112.3 6.2 %slice.241 = bf16[16,160,1280]{2,1,0:T(8,128)(2,1)} slice(bf16[16,200,1280]{2,1,0:T(8,128)(2,1)} %bitcast.162), slice={[0:16], [40:200], [0:1280]} | slice | bytes 13107200 | tf_op jit(solution)/shard_map/slice | solution.py:607
  124.7 4.4 all-to-all-done.2
  130.7 7.9 %collective-permute-done.17 = bf16[128,2560]{1,0:T(8,128)(2,1)} collective-permute-done((bf16[128,2560]{1,0:T(8,128)(2,1)}, bf16[128,2560]{1,0:T(8,128)(2,1)}, u32[]{:S(2)}, u32[]{:S(2)}) %collective-permute-start.17) | collective-permute-done | bytes 655392 | tf_op jit(solution)/shard_map/ppermute | solution.py:43
  140.7 3.3 collective-permute-start.19
  145.3 2.7 collective-permute-done.18
  148.1 6.6 %shard_map.186.attended = bf16[128,1280]{1,0:T(8,128)(2,1)S(1)} custom-call(bf16[128,1280]{1,0:T(8,128)(2,1)S(1)} %multiply_convert_fusion.1, bf16[2,1024,256]{2,1,0:T(8,128)(2,1)S(1)} %bitcast.150, bf16[2,1024,256]{2,1,0:T(8,128)(2,1)S(1)} %bitcast.155, bf16[2,128,256]{2,1,0:T(8,128)(2,1)S(1)} %maximum_select_fusion.refs_2_, ...), custom_call_target="tpu_custom_call" | custom-call | flops 1426063360 | bytes 3997696 | tf_op jit(solution)/shard_map/pallas_call | solution.py:245
  157.0 3.0 collective-permute-start.15
  161.2 26.0 %collective-permute-done.15 = bf16[128,2560]{1,0:T(8,128)(2,1)S(1)} collective-permute-done((bf16[128,2560]{1,0:T(8,128)(2,1)S(1)}, bf16[128,2560]{1,0:T(8,128)(2,1)S(1)}, u32[]{:S(2)}, u32[]{:S(2)}) %collective-permute-start.15) | collective-permute-done | bytes 655392 | tf_op jit(solution)/shard_map/ppermute | solution.py:47
  188.8 3.2 collective-permute-start.20
  192.0 12.1 %collective-permute-done.21 = bf16[128,2560]{1,0:T(8,128)(2,1)S(1)} collective-permute-done((bf16[128,2560]{1,0:T(8,128)(2,1)S(1)}, bf16[128,2560]{1,0:T(8,128)(2,1)S(1)}, u32[]{:S(2)}, u32[]{:S(2)}) %collective-permute-start.21) | collective-permute-done | bytes 655392 | tf_op jit(solution)/shard_map/ppermute | solution.py:43
  204.2 3.7 collective-permute-start.23
  208.8 3.7 collective-permute-done.22
  214.9 15.3 %shard_map.187 = (bf16[512,1024]{1,0:T(8,128)(2,1)}, bf16[512,2048]{1,0:T(8,128)(2,1)}) custom-call(bf16[512,2560]{1,0:T(8,128)(2,1)} %constant_dynamic-update-slice_fusion.5.tokens.refs_0_, bf16[512,2560]{1,0:T(8,128)(2,1)} %copy-done.6, bf16[2560,3072]{1,0:T(8,128)(2,1)} %all-gather.5.cloned.1.call-done.gate_weight.up_weight.down_weight, ...), custom_call_target="tpu_custom_call" | custom-call | flops 8053063680 | bytes 24117248 | tf_op jit(solution)/shard_map/pallas_call | solution.py:310
  233.0 12.0 %shard_map.188 = bf16[2560,3072]{1,0:T(8,128)(2,1)} custom-call(bf16[512,2560]{1,0:T(8,128)(2,1)} %constant_dynamic-update-slice_fusion.5.tokens.refs_0_, bf16[512,2048]{1,0:T(8,128)(2,1)S(1)} %copy-done.31, bf16[512,2560]{1,0:T(8,128)(2,1)S(1)} %copy-done.7, bf16[512,1024]{1,0:T(8,128)(2,1)S(1)} %copy-done.33), custom_call_target="tpu_custom_call" | custom-call | flops 8053063680 | bytes 24117248 | tf_op jit(solution)/shard_map/pallas_call | solution.py:365
  246.5 8.3 %fusion.4 = bf16[512,2560]{1,0:T(8,128)(2,1)S(1)} fusion(bf16[512,2048]{1,0:T(8,128)(2,1)S(1)} %copy-done.32, bf16[2560,3072]{1,0:T(8,128)(2,1)} %all-gather.5.cloned.1.call-done.gate_weight.up_weight.down_weight), kind=kOutput, calls=%fused_computation.4 | convolution fusion | flops 5370019840 | bytes 15204352 | tf_op jit(solution)/shard_map/tf,ef->te/dot_general | solution.py:641
  255.0 3.1 collective-permute-start.24
  258.4 6.6 %collective-permute-done.24 = bf16[64,2560]{1,0:T(8,128)(2,1)S(1)} collective-permute-done((bf16[64,2560]{1,0:T(8,128)(2,1)S(1)}, bf16[64,2560]{1,0:T(8,128)(2,1)S(1)}, u32[]{:S(2)}, u32[]{:S(2)}) %collective-permute-start.24) | collective-permute-done | bytes 327712 | tf_op jit(solution)/shard_map/ppermute | solution.py:43
  265.2 3.8 collective-permute-start.25
  269.3 7.8 %collective-permute-done.25 = bf16[128,2560]{1,0:T(8,128)(2,1)S(1)} collective-permute-done((bf16[128,2560]{1,0:T(8,128)(2,1)S(1)}, bf16[128,2560]{1,0:T(8,128)(2,1)S(1)}, u32[]{:S(2)}, u32[]{:S(2)}) %collective-permute-start.25) | collective-permute-done | bytes 655392 | tf_op jit(solution)/shard_map/ppermute | solution.py:43
  277.1 4.0 collective-permute-done.27
  282.1 2.9 collective-permute-start.28
  288.0 13.8 %collective-permute-done.28 = bf16[128,2560]{1,0:T(8,128)(2,1)} collective-permute-done((bf16[128,2560]{1,0:T(8,128)(2,1)}, bf16[128,2560]{1,0:T(8,128)(2,1)}, u32[]{:S(2)}, u32[]{:S(2)}) %collective-permute-start.28) | collective-permute-done | bytes 655392 | tf_op jit(solution)/shard_map/ppermute | solution.py:47
  303.9 3.6 fusion.44
  309.3 13.4 %shard_map.189 = (bf16[128,2560]{1,0:T(8,128)(2,1)}, bf16[2,8,2,128,256]{4,3,2,1,0:T(8,128)(2,1)}, bf16[2,128,256]{2,1,0:T(8,128)(2,1)}) custom-call(s32[1]{0:T(128)} %bitcast.36.core, bf16[128,1280]{1,0:T(8,128)(2,1)} %copy-done.29, bf16[128,1280]{1,0:T(8,128)(2,1)} %convolution_convert_fusion.out_grad, bf16[128,1280]{1,0:T(8,128)(2,1)} %copy-done.28, ...), custom_call_target="tpu_custom_call" | custom-call | flops 3565158400 | bytes 6553600 | tf_op jit(solution)/shard_map/pallas_call | solution.py:266
  326.4 6.5 %all-to-all-start.4 = ((bf16[32,128,256]{2,1,0:T(8,128)(2,1)}), bf16[32,128,256]{2,1,0:T(8,128)(2,1)}, u32[]{:S(2)}, u32[]{:S(2)}) async-start(bf16[32,128,256]{2,1,0:T(8,128)(2,1)} %bitcast.175), calls=%async_computation.5 | async-start | bytes 4194304 | tf_op jit(solution)/shard_map/all_to_all | solution.py:663
  335.2 9.4 %collective-permute-done.31.refs_8_.refs_3_ = bf16[128,2560]{1,0:T(8,128)(2,1)S(1)} collective-permute-done((bf16[128,2560]{1,0:T(8,128)(2,1)}, bf16[128,2560]{1,0:T(8,128)(2,1)S(1)}, u32[]{:S(2)}, u32[]{:S(2)}) %collective-permute-start.31) | collective-permute-done | bytes 655392 | tf_op jit(solution)/shard_map/ppermute | solution.py:43
  355.3 5.0 %fusion.2 = f32[512,2560]{1,0:T(8,128)S(1)} fusion(bf16[512,1024]{1,0:T(8,128)(2,1)S(1)} %copy-done.34, bf16[2560,3072]{1,0:T(8,128)(2,1)} %all-gather.5.cloned.1.call-done.gate_weight.up_weight.down_weight), kind=kOutput, calls=%fused_computation.2 | convolution fusion | flops 2684354560 | bytes 11534336 | tf_op jit(solution)/shard_map/tf,ef->te/dot_general | solution.py:658
  364.0 4.5 shard_map.190
  374.7 3.1 convert_reduce_fusion.1
  377.9 3.1 fusion.9
  381.0 4.6 all-to-all-start.3
  389.4 5.3 %collective-permute-done.38 = bf16[128,2560]{1,0:T(8,128)(2,1)} collective-permute-done((bf16[128,2560]{1,0:T(8,128)(2,1)}, bf16[128,2560]{1,0:T(8,128)(2,1)}, u32[]{:S(2)}, u32[]{:S(2)}) %collective-permute-start.38) | collective-permute-done | bytes 655392 | tf_op jit(solution)/shard_map/ppermute | solution.py:43
  394.7 2.7 fusion.17
  403.4 3.2 all-to-all-done.3
  407.3 4.2 all-to-all-start.5
  416.5 3.0 collective-permute-start.51
  435.6 9.4 %collective-permute-done.40 = bf16[128,2560]{1,0:T(8,128)(2,1)} collective-permute-done((bf16[128,2560]{1,0:T(8,128)(2,1)}, bf16[128,2560]{1,0:T(8,128)(2,1)}, u32[]{:S(2)}, u32[]{:S(2)}) %collective-permute-start.40) | collective-permute-done | bytes 655392 | tf_op jit(solution)/shard_map/ppermute | solution.py:47
  452.0 5.4 %collective-permute-done.49 = bf16[128,2560]{0,1:T(8,128)(2,1)} collective-permute-done((bf16[128,2560]{0,1:T(8,128)(2,1)}, bf16[128,2560]{0,1:T(8,128)(2,1)}, u32[]{:S(2)}, u32[]{:S(2)}) %collective-permute-start.49) | collective-permute-done | bytes 655392 | tf_op jit(solution)/shard_map/ppermute | solution.py:47
  (395 shorter events, 144.4 us)
Async XLA Ops:
  7.2 86.4 %all-gather.3.cloned.1.call-start = ((), (), s32[]{:S(2)}) async-start(), calls=%async_computation.7 | async-start | bytes 8704000 | tf_op jit(solution)/shard_map/all_gather | solution.py:156
  23.1 191.8 %all-gather.5.cloned.1.call-start = ((), (), s32[]{:S(2)}) async-start(), calls=%async_computation.8 | async-start | bytes 16711680 | tf_op jit(solution)/shard_map/all_gather | solution.py:156
  44.0 11.2 %collective-permute-start = (bf16[128,640]{1,0:T(8,128)(2,1)S(1)}, bf16[128,640]{1,0:T(8,128)(2,1)S(1)}, u32[]{:S(2)}, u32[]{:S(2)}) collective-permute-start(bf16[128,640]{1,0:T(8,128)(2,1)S(1)} %bitcast.184), channel_id=1, source_target_pairs={{0,96},{32,0},{64,32},{96,64},{1,97},{33,1},{65,33},{97,65},{2,98}... | collective-permute-start | bytes 491528 | tf_op jit(solution)/shard_map/ppermute | solution.py:43
  45.2 9.9 %collective-permute-start.1 = (bf16[128,640]{1,0:T(8,128)(2,1)S(1)}, bf16[128,640]{1,0:T(8,128)(2,1)S(1)}, u32[]{:S(2)}, u32[]{:S(2)}) collective-permute-start(bf16[128,640]{1,0:T(8,128)(2,1)S(1)} %bitcast.185), channel_id=1, source_target_pairs={{0,64},{32,96},{64,0},{96,32},{1,65},{33,97},{65,1},{97,33},{2,66}... | collective-permute-start | bytes 491528 | tf_op jit(solution)/shard_map/ppermute | solution.py:43
  46.8 8.4 %collective-permute-start.2 = (bf16[128,640]{1,0:T(8,128)(2,1)S(1)}, bf16[128,640]{1,0:T(8,128)(2,1)S(1)}, u32[]{:S(2)}, u32[]{:S(2)}) collective-permute-start(bf16[128,640]{1,0:T(8,128)(2,1)S(1)} %bitcast.186), channel_id=1, source_target_pairs={{0,32},{32,64},{64,96},{96,0},{1,33},{33,65},{65,97},{97,1},{2,34}... | collective-permute-start | bytes 491528 | tf_op jit(solution)/shard_map/ppermute | solution.py:43
  48.7 19.0 %all-to-all-start.1 = ((bf16[16,40,256]{2,1,0:T(8,128)(2,1)}), bf16[16,40,256]{2,1,0:T(8,128)(2,1)S(1)}, u32[]{:S(2)}, u32[]{:S(2)}) async-start(bf16[16,40,256]{2,1,0:T(8,128)(2,1)} %broadcast_in_dim.118), calls=%async_computation.1 | async-start | bytes 655360 | tf_op jit(solution)/shard_map/all_to_all | solution.py:152
  89.0 10.9 %collective-permute-start.13 = (bf16[128,256]{1,0:T(8,128)(2,1)S(1)}, bf16[128,256]{1,0:T(8,128)(2,1)S(1)}, u32[]{:S(2)}, u32[]{:S(2)}) collective-permute-start(bf16[128,256]{1,0:T(8,128)(2,1)S(1)} %fusion.34), channel_id=1, source_target_pairs={{0,32},{32,64},{64,96},{96,0},{1,33},{33,65},{65,97},{97,1},{2,34}... | collective-permute-start | bytes 196616 | tf_op jit(solution)/shard_map/ppermute | solution.py:43
  96.5 8.8 %collective-permute-start.11 = (bf16[64,1280]{1,0:T(8,128)(2,1)S(1)}, bf16[64,1280]{1,0:T(8,128)(2,1)S(1)}, u32[]{:S(2)}, u32[]{:S(2)}) collective-permute-start(bf16[64,1280]{1,0:T(8,128)(2,1)S(1)} %get-tuple-element.166), channel_id=1, source_target_pairs={{0,32},{32,64},{64,96},{96,0},{1,33},{33,65},{65,97},{97,1},{2,34}... | collective-permute-start | bytes 491528 | tf_op jit(solution)/shard_map/ppermute | solution.py:43
  96.7 8.7 %collective-permute-start.9 = (bf16[64,1280]{1,0:T(8,128)(2,1)S(1)}, bf16[64,1280]{1,0:T(8,128)(2,1)}, u32[]{:S(2)}, u32[]{:S(2)}) collective-permute-start(bf16[64,1280]{1,0:T(8,128)(2,1)S(1)} %get-tuple-element.165), channel_id=1, source_target_pairs={{0,96},{32,0},{64,32},{96,64},{1,97},{33,1},{65,33},{97,65},{2,98}... | collective-permute-start | bytes 491528 | tf_op jit(solution)/shard_map/ppermute | solution.py:43
  101.0 28.1 %all-to-all-start.2 = ((bf16[16,128,256]{2,1,0:T(8,128)(2,1)}), bf16[16,128,256]{2,1,0:T(8,128)(2,1)S(1)}, u32[]{:S(2)}, u32[]{:S(2)}) async-start(bf16[16,128,256]{2,1,0:T(8,128)(2,1)} %bitcast.22), calls=%async_computation.2 | async-start | bytes 2097152 | tf_op jit(solution)/shard_map/all_to_all | solution.py:618
  105.3 301.3 %reduce-scatter.2.cloned.1.call-start = ((), (), s32[]{:S(2)}) async-start(), calls=%async_computation.9 | async-start | bytes 16711680 | tf_op jit(solution)/shard_map/reduce_scatter | solution.py:639
  107.6 10.9 %collective-permute-start.10 = (bf16[128,1280]{1,0:T(8,128)(2,1)}, bf16[128,1280]{1,0:T(8,128)(2,1)}, u32[]{:S(2)}, u32[]{:S(2)}) collective-permute-start(bf16[128,1280]{1,0:T(8,128)(2,1)} %fusion.26), channel_id=1, source_target_pairs={{0,96},{32,0},{64,32},{96,64},{1,97},{33,1},{65,33},{97,65},{2,98}... | collective-permute-start | bytes 983048 | tf_op jit(solution)/shard_map/ppermute | solution.py:43
  109.6 8.8 %collective-permute-start.12 = (bf16[128,1280]{1,0:T(8,128)(2,1)}, bf16[128,1280]{1,0:T(8,128)(2,1)}, u32[]{:S(2)}, u32[]{:S(2)}) collective-permute-start(bf16[128,1280]{1,0:T(8,128)(2,1)} %fusion.27), channel_id=1, source_target_pairs={{0,32},{32,64},{64,96},{96,0},{1,33},{33,65},{65,97},{97,1},{2,34}... | collective-permute-start | bytes 983048 | tf_op jit(solution)/shard_map/ppermute | solution.py:43
  122.2 17.5 %collective-permute-start.16 = (bf16[128,2560]{1,0:T(8,128)(2,1)}, bf16[128,2560]{1,0:T(8,128)(2,1)}, u32[]{:S(2)}, u32[]{:S(2)}) collective-permute-start(bf16[128,2560]{1,0:T(8,128)(2,1)} %copy.68), channel_id=1, source_target_pairs={{0,96},{32,0},{64,32},{96,64},{1,97},{33,1},{65,33},{97,65},{2,98}... | collective-permute-start | bytes 1966088 | tf_op jit(solution)/shard_map/ppermute | solution.py:43
  124.7 13.9 %collective-permute-start.17 = (bf16[128,2560]{1,0:T(8,128)(2,1)}, bf16[128,2560]{1,0:T(8,128)(2,1)}, u32[]{:S(2)}, u32[]{:S(2)}) collective-permute-start(bf16[128,2560]{1,0:T(8,128)(2,1)} %copy.68), channel_id=1, source_target_pairs={{0,32},{32,64},{64,96},{96,0},{1,33},{33,65},{65,97},{97,1},{2,34}... | collective-permute-start | bytes 1966088 | tf_op jit(solution)/shard_map/ppermute | solution.py:43
  129.3 18.7 %collective-permute-start.14 = (bf16[2,8,128,256]{3,2,1,0:T(8,128)(2,1)S(1)}, bf16[2,8,128,256]{3,2,1,0:T(8,128)(2,1)S(1)}, u32[]{:S(2)}, u32[]{:S(2)}) collective-permute-start(bf16[2,8,128,256]{3,2,1,0:T(8,128)(2,1)S(1)} %broadcast_select_fusion), channel_id=1, source_target_pairs={{0,2},{2,0},{1,3},{3,1},{4,6},{6,4},{5,7},{7,5},{8,10},{10,8},{9,1... | collective-permute-start | bytes 3145736 | tf_op jit(solution)/shard_map/ppermute | solution.py:51
  140.7 19.3 %collective-permute-start.19 = (bf16[64,2560]{1,0:T(8,128)(2,1)S(1)}, bf16[64,2560]{1,0:T(8,128)(2,1)S(1)}, u32[]{:S(2)}, u32[]{:S(2)}) collective-permute-start(bf16[64,2560]{1,0:T(8,128)(2,1)S(1)} %slice.246), channel_id=1, source_target_pairs={{0,96},{32,0},{64,32},{96,64},{1,97},{33,1},{65,33},{97,65},{2,98}... | collective-permute-start | bytes 983048 | tf_op jit(solution)/shard_map/ppermute | solution.py:43
  157.0 30.2 %collective-permute-start.15 = (bf16[128,2560]{1,0:T(8,128)(2,1)S(1)}, bf16[128,2560]{1,0:T(8,128)(2,1)S(1)}, u32[]{:S(2)}, u32[]{:S(2)}) collective-permute-start(bf16[128,2560]{1,0:T(8,128)(2,1)S(1)} %fusion.7), channel_id=1, source_target_pairs={{0,1},{1,0},{2,3},{3,2},{4,5},{5,4},{6,7},{7,6},{8,9},{9,8},{10,11... | collective-permute-start | bytes 1966088 | tf_op jit(solution)/shard_map/ppermute | solution.py:47
  188.8 15.3 %collective-permute-start.21 = (bf16[128,2560]{1,0:T(8,128)(2,1)S(1)}, bf16[128,2560]{1,0:T(8,128)(2,1)S(1)}, u32[]{:S(2)}, u32[]{:S(2)}) collective-permute-start(bf16[128,2560]{1,0:T(8,128)(2,1)S(1)} %get-tuple-element.115), channel_id=1, source_target_pairs={{0,32},{32,64},{64,96},{96,0},{1,33},{33,65},{65,97},{97,1},{2,34}... | collective-permute-start | bytes 1966088 | tf_op jit(solution)/shard_map/ppermute | solution.py:43
  188.8 15.4 %collective-permute-start.20 = (bf16[128,2560]{1,0:T(8,128)(2,1)S(1)}, bf16[128,2560]{1,0:T(8,128)(2,1)S(1)}, u32[]{:S(2)}, u32[]{:S(2)}) collective-permute-start(bf16[128,2560]{1,0:T(8,128)(2,1)S(1)} %get-tuple-element.115), channel_id=1, source_target_pairs={{0,96},{32,0},{64,32},{96,64},{1,97},{33,1},{65,33},{97,65},{2,98}... | collective-permute-start | bytes 1966088 | tf_op jit(solution)/shard_map/ppermute | solution.py:43
  204.2 9.0 %collective-permute-start.23 = (bf16[64,2560]{1,0:T(8,128)(2,1)S(1)}, bf16[64,2560]{1,0:T(8,128)(2,1)S(1)}, u32[]{:S(2)}, u32[]{:S(2)}) collective-permute-start(bf16[64,2560]{1,0:T(8,128)(2,1)S(1)} %slice.248), channel_id=1, source_target_pairs={{0,96},{32,0},{64,32},{96,64},{1,97},{33,1},{65,33},{97,65},{2,98}... | collective-permute-start | bytes 983048 | tf_op jit(solution)/shard_map/ppermute | solution.py:43
  255.0 10.1 %collective-permute-start.24 = (bf16[64,2560]{1,0:T(8,128)(2,1)S(1)}, bf16[64,2560]{1,0:T(8,128)(2,1)S(1)}, u32[]{:S(2)}, u32[]{:S(2)}) collective-permute-start(bf16[64,2560]{1,0:T(8,128)(2,1)S(1)} %get-tuple-element.152), channel_id=1, source_target_pairs={{0,96},{32,0},{64,32},{96,64},{1,97},{33,1},{65,33},{97,65},{2,98}... | collective-permute-start | bytes 983048 | tf_op jit(solution)/shard_map/ppermute | solution.py:43
  258.4 10.7 %collective-permute-start.26 = (bf16[64,2560]{1,0:T(8,128)(2,1)S(1)}, bf16[64,2560]{1,0:T(8,128)(2,1)S(1)}, u32[]{:S(2)}, u32[]{:S(2)}) collective-permute-start(bf16[64,2560]{1,0:T(8,128)(2,1)S(1)} %get-tuple-element.153), channel_id=1, source_target_pairs={{0,32},{32,64},{64,96},{96,0},{1,33},{33,65},{65,97},{97,1},{2,34}... | collective-permute-start | bytes 983048 | tf_op jit(solution)/shard_map/ppermute | solution.py:43
  265.2 11.9 %collective-permute-start.25 = (bf16[128,2560]{1,0:T(8,128)(2,1)S(1)}, bf16[128,2560]{1,0:T(8,128)(2,1)S(1)}, u32[]{:S(2)}, u32[]{:S(2)}) collective-permute-start(bf16[128,2560]{1,0:T(8,128)(2,1)S(1)} %fusion.18), channel_id=1, source_target_pairs={{0,96},{32,0},{64,32},{96,64},{1,97},{33,1},{65,33},{97,65},{2,98}... | collective-permute-start | bytes 1966088 | tf_op jit(solution)/shard_map/ppermute | solution.py:43
  269.2 11.9 %collective-permute-start.27 = (bf16[128,2560]{1,0:T(8,128)(2,1)S(1)}, bf16[128,2560]{1,0:T(8,128)(2,1)S(1)}, u32[]{:S(2)}, u32[]{:S(2)}) collective-permute-start(bf16[128,2560]{1,0:T(8,128)(2,1)S(1)} %fusion.19), channel_id=1, source_target_pairs={{0,32},{32,64},{64,96},{96,0},{1,33},{33,65},{65,97},{97,1},{2,34}... | collective-permute-start | bytes 1966088 | tf_op jit(solution)/shard_map/ppermute | solution.py:43
  282.1 19.7 %collective-permute-start.28 = (bf16[128,2560]{1,0:T(8,128)(2,1)}, bf16[128,2560]{1,0:T(8,128)(2,1)}, u32[]{:S(2)}, u32[]{:S(2)}) collective-permute-start(bf16[128,2560]{1,0:T(8,128)(2,1)} %reduce-precision_convert_fusion.1), channel_id=1, source_target_pairs={{0,1},{1,0},{2,3},{3,2},{4,5},{5,4},{6,7},{7,6},{8,9},{9,8},{10,11... | collective-permute-start | bytes 1966088 | tf_op jit(solution)/shard_map/ppermute | solution.py:47
  322.7 10.8 %collective-permute-start.29 = (bf16[128,2560]{1,0:T(8,128)(2,1)}, bf16[128,2560]{1,0:T(8,128)(2,1)S(1)}, u32[]{:S(2)}, u32[]{:S(2)}) collective-permute-start(bf16[128,2560]{1,0:T(8,128)(2,1)} %get-tuple-element.65.refs_5_.refs_0_), channel_id=1, source_target_pairs={{0,96},{32,0},{64,32},{96,64},{1,97},{33,1},{65,33},{97,65},{2,98}... | collective-permute-start | bytes 1966088 | tf_op jit(solution)/shard_map/ppermute | solution.py:43
  322.7 12.5 %collective-permute-start.30 = (bf16[128,2560]{1,0:T(8,128)(2,1)}, bf16[128,2560]{1,0:T(8,128)(2,1)S(1)}, u32[]{:S(2)}, u32[]{:S(2)}) collective-permute-start(bf16[128,2560]{1,0:T(8,128)(2,1)} %get-tuple-element.65.refs_5_.refs_0_), channel_id=1, source_target_pairs={{0,64},{32,96},{64,0},{96,32},{1,65},{33,97},{65,1},{97,33},{2,66}... | collective-permute-start | bytes 1966088 | tf_op jit(solution)/shard_map/ppermute | solution.py:43
  323.6 20.9 %collective-permute-start.31 = (bf16[128,2560]{1,0:T(8,128)(2,1)}, bf16[128,2560]{1,0:T(8,128)(2,1)S(1)}, u32[]{:S(2)}, u32[]{:S(2)}) collective-permute-start(bf16[128,2560]{1,0:T(8,128)(2,1)} %get-tuple-element.65.refs_5_.refs_0_), channel_id=1, source_target_pairs={{0,32},{32,64},{64,96},{96,0},{1,33},{33,65},{65,97},{97,1},{2,34}... | collective-permute-start | bytes 1966088 | tf_op jit(solution)/shard_map/ppermute | solution.py:43
  324.7 60.9 %collective-permute-start.42 = (f32[1,128]{1,0:T(1,128)S(1)}, f32[1,128]{1,0:T(1,128)S(1)}, u32[]{:S(2)}, u32[]{:S(2)}) collective-permute-start(f32[1,128]{1,0:T(1,128)S(1)} %bitcast.199), channel_id=1, source_target_pairs={{0,32},{32,64},{64,96},{96,0},{1,33},{33,65},{65,97},{97,1},{2,34}... | collective-permute-start | bytes 1544 | tf_op jit(solution)/shard_map/ppermute | solution.py:43
  326.4 48.3 %all-to-all-start.4 = ((bf16[32,128,256]{2,1,0:T(8,128)(2,1)}), bf16[32,128,256]{2,1,0:T(8,128)(2,1)}, u32[]{:S(2)}, u32[]{:S(2)}) async-start(bf16[32,128,256]{2,1,0:T(8,128)(2,1)} %bitcast.175), calls=%async_computation.5 | async-start | bytes 4194304 | tf_op jit(solution)/shard_map/all_to_all | solution.py:663
  346.8 8.4 %collective-permute-start.34 = (bf16[640,128]{1,0:T(8,128)(2,1)S(1)}, bf16[640,128]{1,0:T(8,128)(2,1)S(1)}, u32[]{:S(2)}, u32[]{:S(2)}) collective-permute-start(bf16[640,128]{1,0:T(8,128)(2,1)S(1)} %get-tuple-element.148), channel_id=1, source_target_pairs={{0,32},{32,64},{64,96},{96,0},{1,33},{33,65},{65,97},{97,1},{2,34}... | collective-permute-start | bytes 491528 | tf_op jit(solution)/shard_map/ppermute | solution.py:43
  348.8 36.9 %collective-permute-start.41 = (bf16[128,256]{1,0:T(8,128)(2,1)}, bf16[128,256]{1,0:T(8,128)(2,1)S(1)}, u32[]{:S(2)}, u32[]{:S(2)}) collective-permute-start(bf16[128,256]{1,0:T(8,128)(2,1)} %select_bitcast_fusion), channel_id=1, source_target_pairs={{0,1},{1,0},{2,3},{3,2},{4,5},{5,4},{6,7},{7,6},{8,9},{9,8},{10,11... | collective-permute-start | bytes 196616 | tf_op jit(solution)/shard_map/ppermute | solution.py:47
  360.4 9.6 %collective-permute-start.35 = (bf16[64,2560]{1,0:T(8,128)(2,1)S(1)}, bf16[64,2560]{1,0:T(8,128)(2,1)S(1)}, u32[]{:S(2)}, u32[]{:S(2)}) collective-permute-start(bf16[64,2560]{1,0:T(8,128)(2,1)S(1)} %get-tuple-element.146), channel_id=1, source_target_pairs={{0,96},{32,0},{64,32},{96,64},{1,97},{33,1},{65,33},{97,65},{2,98}... | collective-permute-start | bytes 983048 | tf_op jit(solution)/shard_map/ppermute | solution.py:43
  371.8 17.6 %collective-permute-start.36 = (bf16[128,2560]{1,0:T(8,128)(2,1)}, bf16[128,2560]{1,0:T(8,128)(2,1)}, u32[]{:S(2)}, u32[]{:S(2)}) collective-permute-start(bf16[128,2560]{1,0:T(8,128)(2,1)} %fusion.20), channel_id=1, source_target_pairs={{0,96},{32,0},{64,32},{96,64},{1,97},{33,1},{65,33},{97,65},{2,98}... | collective-permute-start | bytes 1966088 | tf_op jit(solution)/shard_map/ppermute | solution.py:43
  374.0 20.7 %collective-permute-start.38 = (bf16[128,2560]{1,0:T(8,128)(2,1)}, bf16[128,2560]{1,0:T(8,128)(2,1)}, u32[]{:S(2)}, u32[]{:S(2)}) collective-permute-start(bf16[128,2560]{1,0:T(8,128)(2,1)} %fusion.21), channel_id=1, source_target_pairs={{0,32},{32,64},{64,96},{96,0},{1,33},{33,65},{65,97},{97,1},{2,34}... | collective-permute-start | bytes 1966088 | tf_op jit(solution)/shard_map/ppermute | solution.py:43
  381.0 25.6 %all-to-all-start.3 = ((bf16[8,40,2560]{2,1,0:T(8,128)(2,1)}), bf16[8,40,2560]{2,1,0:T(8,128)(2,1)S(1)}, u32[]{:S(2)}, u32[]{:S(2)}) async-start(bf16[8,40,2560]{2,1,0:T(8,128)(2,1)} %fusion.9), calls=%async_computation.4 | async-start | bytes 3276800 | tf_op jit(solution)/shard_map/all_to_all | solution.py:685
  385.8 11.6 %collective-permute-start.43 = (bf16[256,256]{1,0:T(8,128)(2,1)S(1)}, bf16[256,256]{1,0:T(8,128)(2,1)S(1)}, u32[]{:S(2)}, u32[]{:S(2)}) collective-permute-start(bf16[256,256]{1,0:T(8,128)(2,1)S(1)} %fusion.28.refs_4_), channel_id=1, source_target_pairs={{0,96},{32,0},{64,32},{96,64},{1,97},{33,1},{65,33},{97,65},{2,98}... | collective-permute-start | bytes 393224 | tf_op jit(solution)/shard_map/ppermute | solution.py:43
  388.5 8.9 %collective-permute-start.44 = (bf16[256,256]{1,0:T(8,128)(2,1)S(1)}, bf16[256,256]{1,0:T(8,128)(2,1)S(1)}, u32[]{:S(2)}, u32[]{:S(2)}) collective-permute-start(bf16[256,256]{1,0:T(8,128)(2,1)S(1)} %fusion.28.refs_4_), channel_id=1, source_target_pairs={{0,64},{32,96},{64,0},{96,32},{1,65},{33,97},{65,1},{97,33},{2,66}... | collective-permute-start | bytes 393224 | tf_op jit(solution)/shard_map/ppermute | solution.py:43
  388.9 9.0 %collective-permute-start.45 = (bf16[256,256]{1,0:T(8,128)(2,1)S(1)}, bf16[256,256]{1,0:T(8,128)(2,1)S(1)}, u32[]{:S(2)}, u32[]{:S(2)}) collective-permute-start(bf16[256,256]{1,0:T(8,128)(2,1)S(1)} %fusion.28.refs_4_), channel_id=1, source_target_pairs={{0,32},{32,64},{64,96},{96,0},{1,33},{33,65},{65,97},{97,1},{2,34}... | collective-permute-start | bytes 393224 | tf_op jit(solution)/shard_map/ppermute | solution.py:43
  400.4 12.1 %collective-permute-start.47 = (bf16[128,640]{1,0:T(8,128)(2,1)S(1)}, bf16[128,640]{1,0:T(8,128)(2,1)S(1)}, u32[]{:S(2)}, u32[]{:S(2)}) collective-permute-start(bf16[128,640]{1,0:T(8,128)(2,1)S(1)} %get-tuple-element.76), channel_id=1, source_target_pairs={{0,64},{32,96},{64,0},{96,32},{1,65},{33,97},{65,1},{97,33},{2,66}... | collective-permute-start | bytes 491528 | tf_op jit(solution)/shard_map/ppermute | solution.py:43
  401.1 11.4 %collective-permute-start.48 = (bf16[128,640]{1,0:T(8,128)(2,1)S(1)}, bf16[128,640]{1,0:T(8,128)(2,1)S(1)}, u32[]{:S(2)}, u32[]{:S(2)}) collective-permute-start(bf16[128,640]{1,0:T(8,128)(2,1)S(1)} %get-tuple-element.77), channel_id=1, source_target_pairs={{0,96},{32,0},{64,32},{96,64},{1,97},{33,1},{65,33},{97,65},{2,98}... | collective-permute-start | bytes 491528 | tf_op jit(solution)/shard_map/ppermute | solution.py:43
  407.3 21.7 %all-to-all-start.5 = ((bf16[16,40,256]{2,1,0:T(8,128)(2,1)}), bf16[16,40,256]{2,1,0:T(8,128)(2,1)}, u32[]{:S(2)}, u32[]{:S(2)}) async-start(bf16[16,40,256]{2,1,0:T(8,128)(2,1)} %bitcast.84), calls=%async_computation.6 | async-start | bytes 655360 | tf_op jit(solution)/shard_map/all_to_all | solution.py:699
  416.4 13.6 %collective-permute-start.50 = (bf16[40,3072]{1,0:T(8,128)(2,1)}, bf16[40,3072]{1,0:T(8,128)(2,1)S(1)}, u32[]{:S(2)}, u32[]{:S(2)}) collective-permute-start(bf16[40,3072]{1,0:T(8,128)(2,1)} %get-tuple-element.141), channel_id=1, source_target_pairs={{0,32},{32,64},{64,96},{96,0},{1,33},{33,65},{65,97},{97,1},{2,34}... | collective-permute-start | bytes 737288 | tf_op jit(solution)/shard_map/ppermute | solution.py:43
  416.5 14.5 %collective-permute-start.51 = (bf16[40,3072]{1,0:T(8,128)(2,1)}, bf16[40,3072]{1,0:T(8,128)(2,1)}, u32[]{:S(2)}, u32[]{:S(2)}) collective-permute-start(bf16[40,3072]{1,0:T(8,128)(2,1)} %get-tuple-element.140), channel_id=1, source_target_pairs={{0,64},{32,96},{64,0},{96,32},{1,65},{33,97},{65,1},{97,33},{2,66}... | collective-permute-start | bytes 737288 | tf_op jit(solution)/shard_map/ppermute | solution.py:43
  419.5 11.5 %collective-permute-start.52 = (bf16[40,3072]{1,0:T(8,128)(2,1)}, bf16[40,3072]{1,0:T(8,128)(2,1)}, u32[]{:S(2)}, u32[]{:S(2)}) collective-permute-start(bf16[40,3072]{1,0:T(8,128)(2,1)} %get-tuple-element.139), channel_id=1, source_target_pairs={{0,96},{32,0},{64,32},{96,64},{1,97},{33,1},{65,33},{97,65},{2,98}... | collective-permute-start | bytes 737288 | tf_op jit(solution)/shard_map/ppermute | solution.py:43
  425.4 19.6 %collective-permute-start.40 = (bf16[128,2560]{1,0:T(8,128)(2,1)}, bf16[128,2560]{1,0:T(8,128)(2,1)}, u32[]{:S(2)}, u32[]{:S(2)}) collective-permute-start(bf16[128,2560]{1,0:T(8,128)(2,1)} %fusion.17), channel_id=1, source_target_pairs={{0,1},{1,0},{2,3},{3,2},{4,5},{5,4},{6,7},{7,6},{8,9},{9,8},{10,11... | collective-permute-start | bytes 1966088 | tf_op jit(solution)/shard_map/ppermute | solution.py:47
  426.7 30.7 %collective-permute-start.49 = (bf16[128,2560]{0,1:T(8,128)(2,1)}, bf16[128,2560]{0,1:T(8,128)(2,1)}, u32[]{:S(2)}, u32[]{:S(2)}) collective-permute-start(bf16[128,2560]{0,1:T(8,128)(2,1)} %reduce-precision_convert_fusion), channel_id=1, source_target_pairs={{0,1},{1,0},{2,3},{3,2},{4,5},{5,4},{6,7},{7,6},{8,9},{9,8},{10,11... | collective-permute-start | bytes 1966088 | tf_op jit(solution)/shard_map/ppermute | solution.py:47
  (91 other events, 1066.9 us)
Sparse Core Ops, SparseCore 0:
  23.2 57.0 all-gather.2
  81.9 112.9 all-gather.4
  245.1 134.3 reduce-scatter.1
where the time goes:
time: 484 us; the launch traced here: 474 us
  waiting for transfers between devices  156 us (32%)
  starting transfers between devices  101 us (21%)
  Pallas kernels  57.6 us (12%)
  local copies, waits for them, and re-layouts  53.4 us (11%)
  other arithmetic  41.9 us (9%)
  blocking collectives  29.5 us (6%)
  matrix products  18.9 us (4%)
  between operations  15.8 us (3%)
    ppermute x45, waiting for transfers between devices, to_plane(): lax.ppermute(block, X, [(i, (i + shift) % PLANES) for i in range(PLANES)])  81.8 us
    ppermute x8, waiting for transfers between devices, swap(): return lax.ppermute(block, M, [(0, 1), (1, 0)])  57.1 us
    ppermute x45, starting transfers between devices, to_plane(): lax.ppermute(block, X, [(i, (i + shift) % PLANES) for i in range(PLANES)])  56.2 us
    ppermute x8, starting transfers between devices, swap(): return lax.ppermute(block, M, [(0, 1), (1, 0)])  18.4 us
    unnamed x166, local copies, waits for them, and re-layouts  16.9 us
    all_to_all x1, blocking collectives, body(): ffn_own = lax.all_to_all(after(ffn_own, out_planes), X, 0, 0, tiled=True)  16.2 us
    pallas_call x1, Pallas kernels, geglu(): pl.pallas_call(geglu_kernel, grid=(steps,), in_specs=[token_spec, token_s...  15.3 us
    pallas_call x1, Pallas kernels, attend_back(): pl.pallas_call(attend_back_kernel, grid=(heads,), in_specs=[pl.BlockSpec(...  13.4 us
  transfers between devices with their start and end apart: 63, of which 30 were waited for; matrix products, arithmetic and copies ran while one was open for 21% of the time, Pallas kernels for 6%

commit v1 on v0

--- a/solution.py
+++ b/solution.py
@@ -281,24 +281,41 @@
     )(core.reshape(1), queries, out_grad, attended, token_scale, *parts, *biases)
 
 
-def geglu_kernel(tokens, cot, gate_weight, up_weight, down_weight, hidden, gate_up):
+def geglu_kernel(
+    steps, tokens, cot, gate_weight, up_weight, down_weight, hidden, gate_up, grads
+):
     step = pl.program_id(0)
     block = gate_weight.shape[1]
-    gate = jnp.dot(tokens[...], gate_weight[...], preferred_element_type=F32)
-    up = jnp.dot(tokens[...], up_weight[...], preferred_element_type=F32)
-    hidden_grad = jnp.dot(cot[...], down_weight[...], preferred_element_type=F32)
-    hidden_grad = hidden_grad.astype(BF16).astype(F32)
-    root = 0.7978845608028654
-    square = gate * gate
-    bend = jnp.tanh(root * gate * (1.0 + 0.044715 * square))
-    half = 0.5 * (1.0 + bend)
-    gelu = gate * half
-    slope = half + 0.5 * gate * (1.0 - bend * bend) * (root * (1.0 + 3 * 0.044715 * square))
-    here = pl.ds(pl.multiple_of(step * block, block), block)
-    hidden[:, here] = (gelu * up).astype(BF16)
-    gate_up[:, here] = (hidden_grad * up * slope).astype(BF16)
-    there = pl.ds(pl.multiple_of(hidden.shape[1] + step * block, block), block)
-    gate_up[:, there] = (hidden_grad * gelu).astype(BF16)
+    units = hidden.shape[1]
+
+    @pl.when(step < steps)
+    def _():
+        gate = jnp.dot(tokens[...], gate_weight[...], preferred_element_type=F32)
+        up = jnp.dot(tokens[...], up_weight[...], preferred_element_type=F32)
+        hidden_grad = jnp.dot(cot[...], down_weight[...], preferred_element_type=F32)
+        hidden_grad = hidden_grad.astype(BF16).astype(F32)
+        root = 0.7978845608028654
+        square = gate * gate
+        bend = jnp.tanh(root * gate * (1.0 + 0.044715 * square))
+        half = 0.5 * (1.0 + bend)
+        gelu = gate * half
+        slope = half + 0.5 * gate * (1.0 - bend * bend) * (root * (1.0 + 3 * 0.044715 * square))
+        here = pl.ds(pl.multiple_of(step * block, block), block)
+        hidden[:, here] = (gelu * up).astype(BF16)
+        gate_up[:, here] = (hidden_grad * up * slope).astype(BF16)
+        there = pl.ds(pl.multiple_of(units + step * block, block), block)
+        gate_up[:, there] = (hidden_grad * gelu).astype(BF16)
+
+    @pl.when(step >= steps)
+    def _():
+        height = grads.shape[0]
+        rows = pl.ds(pl.multiple_of((step - steps) * height, 128), height)
+        cut = 512 if units % 512 == 0 else 128
+        for left, right, first in ((tokens, gate_up, 0), (cot, hidden, 2 * units)):
+            for at in range(0, right.shape[1], cut):
+                grads[:, first + at : first + at + cut] = dot_tokens(
+                    left[:, rows], right[:, at : at + cut]
+                ).astype(BF16)
 
 
 def geglu(tokens, cot, weights):
@@ -306,26 +323,32 @@
     units = weights.shape[1] // 3
     block = 256 if units % 256 == 0 else 128
     steps = units // block
+    height = width // PLANES
     token_spec = pl.BlockSpec(tokens.shape, lambda i: (0, 0), pipeline_mode=pl.Buffered(1))
+
+    def weight_spec(which):
+        return pl.BlockSpec(
+            (width, block), lambda i: (0, which * steps + jnp.minimum(i, steps - 1))
+        )
+
     return pl.pallas_call(
-        geglu_kernel,
-        grid=(steps,),
-        in_specs=[
-            token_spec,
-            token_spec,
-            pl.BlockSpec((width, block), lambda i: (0, i)),
-            pl.BlockSpec((width, block), lambda i: (0, steps + i)),
-            pl.BlockSpec((width, block), lambda i: (0, 2 * steps + i)),
+        functools.partial(geglu_kernel, steps),
+        grid=(steps + PLANES,),
+        in_specs=[token_spec, token_spec] + [weight_spec(which) for which in range(3)],
+        out_specs=[
+            whole_spec((rows, units)),
+            whole_spec((rows, 2 * units)),
+            pl.BlockSpec((height, 3 * units), lambda i: (jnp.maximum(i - steps, 0), 0)),
         ],
-        out_specs=[whole_spec((rows, units)), whole_spec((rows, 2 * units))],
         out_shape=[
             jax.ShapeDtypeStruct((rows, units), BF16),
             jax.ShapeDtypeStruct((rows, 2 * units), BF16),
+            jax.ShapeDtypeStruct((width, 3 * units), BF16),
         ],
-        compiler_params=pltpu.CompilerParams(vmem_limit_bytes=56 * 1024 * 1024),
+        compiler_params=pltpu.CompilerParams(vmem_limit_bytes=60 * 1024 * 1024),
         cost_estimate=pl.CostEstimate(
-            flops=2 * rows * width * 3 * units,
-            bytes_accessed=2 * weights.size + 4 * tokens.size + 6 * rows * units,
+            flops=4 * rows * width * 3 * units,
+            bytes_accessed=4 * weights.size + 4 * tokens.size + 6 * rows * units,
             transcendentals=rows * units,
         ),
     )(tokens, cot, weights, weights, weights)
@@ -634,10 +657,8 @@
     scale_ffn = rms_scale(middle)
     normed = (middle * scale_ffn).astype(BF16)
     normed_all = gather_planes(normed)
-    hidden, gate_up_low = geglu(normed_all, cot_all, ffn)
-    ffn_grad_part = token_outer((normed_all, gate_up_low), (cot_all, hidden))
+    hidden, gate_up_low, ffn_grad_part = geglu(normed_all, cot_all, ffn)
     ffn_grad_rows = lax.psum_scatter(ffn_grad_part, R, scatter_dimension=0, tiled=True)
-    gate_up_low = after(gate_up_low, ffn_grad_part)
     weighted_part = jnp.einsum(
         "tf,ef->te", gate_up_low, ffn[:, : 2 * padded], preferred_element_type=F32
     ).astype(BF16)
@@ -689,8 +710,7 @@
     ffn_grad_rows, middle_late, ffn_low, attn_met = lax.optimization_barrier(
         (ffn_grad_rows, middle_grad, ffn_low, attn_met)
     )
-    input_parts[1] = after(input_parts[1], attn_met)
-    weighted_low = rounded(join_planes(input_parts).astype(F32))
+    weighted_low = after(rounded(join_planes(input_parts).astype(F32)), attn_met)
     weighted_other = swap(weighted_low)
     ffn_grad_rows = after(ffn_grad_rows, weighted_low)
     attn_base = jnp.sum(attn_met.reshape(CHIPS, own, attn_width).astype(F32), 0)

time: 484 us -> 471 us (0.973)
  the two profiles are of different devices: /device:TPU:0 before, /device:TPU:1 now
where the time goes in v1:
time: 471 us; the launch traced here: 461 us
  starting transfers between devices  132 us (28%)
  waiting for transfers between devices  120 us (25%)
  Pallas kernels  57.2 us (12%)
  local copies, waits for them, and re-layouts  49.3 us (10%)
  other arithmetic  40.8 us (9%)
  blocking collectives  26.6 us (6%)
  matrix products  18.8 us (4%)
  between operations  15.8 us (3%)
    ppermute x45, waiting for transfers between devices, to_plane(): lax.ppermute(block, X, [(i, (i + shift) % PLANES) for i in range(PLANES)])  59 us
    ppermute x45, starting transfers between devices, to_plane(): lax.ppermute(block, X, [(i, (i + shift) % PLANES) for i in range(PLANES)])  50.1 us
    ppermute x8, waiting for transfers between devices, swap(): return lax.ppermute(block, M, [(0, 1), (1, 0)])  46.5 us
    pallas_call x1, Pallas kernels, geglu(): pl.pallas_call(functools.partial(geglu_kernel, steps), grid=(steps + PLAN...  25.9 us
    all_to_all x1, starting transfers between devices, body(): lax.all_to_all(window_grad.reshape(2 * RANKS * rows, HD), (M,) + R, 0, 0,...  21.9 us
    ppermute x8, starting transfers between devices, swap(): return lax.ppermute(block, M, [(0, 1), (1, 0)])  17.5 us
    ppermute x2, starting transfers between devices, swap_cores(): return lax.ppermute(block, CORE, [(0, 1), (1, 0)])  17.1 us
    unnamed x142, local copies, waits for them, and re-layouts  14.6 us
  transfers between devices with their start and end apart: 63, of which 25 were waited for; matrix products, arithmetic and copies ran while one was open for 21% of the time, Pallas kernels for 7%

profile of v1, /device:TPU:1, one launch (start us, length us, event | category | flops | bytes accessed | tf_op | source)
XLA Modules:
  0.0 461.2 jit_solution(1045108302647200312)
XLA Ops:
  7.3 12.3 %all_gather.9 = bf16[160,1280]{1,0:T(8,128)(2,1)S(1)} all-gather(bf16[40,1280]{1,0:T(8,128)(2,1)} %bitcast.186), channel_id=1, replica_groups=mesh['x'=4,'yl'=2,'z'=4,'c'=2,'mp'=2] {'x'}, dimensions={0}, use_global_device_ids=true | all-gather | bytes 512000 | tf_op jit(solution)/shard_map/all_gather | solution.py:563
  25.1 14.3 %all_to_all.56 = bf16[4,40,3072]{2,1,0:T(8,128)(2,1)} all-to-all(bf16[4,40,3072]{2,1,0:T(8,128)(2,1)S(1)} %copy.55), channel_id=1, replica_groups=mesh['x'=4,'yl'=2,'z'=4,'c'=2,'mp'=2] {'x'}, dimensions={0} | all-to-all | bytes 1966080 | tf_op jit(solution)/shard_map/all_to_all | solution.py:565
  45.2 11.2 %all-to-all-start.1 = ((bf16[16,40,256]{2,1,0:T(8,128)(2,1)}), bf16[16,40,256]{2,1,0:T(8,128)(2,1)S(1)}, u32[]{:S(2)}, u32[]{:S(2)}) async-start(bf16[16,40,256]{2,1,0:T(8,128)(2,1)} %broadcast_in_dim.118), calls=%async_computation.1 | async-start | bytes 655360 | tf_op jit(solution)/shard_map/all_to_all | solution.py:152
  59.2 9.0 %all-to-all-done.1 = bf16[16,40,256]{2,1,0:T(8,128)(2,1)S(1)} async-done(((bf16[16,40,256]{2,1,0:T(8,128)(2,1)}), bf16[16,40,256]{2,1,0:T(8,128)(2,1)S(1)}, u32[]{:S(2)}, u32[]{:S(2)}) %all-to-all-start.1) | async-done | bytes 327712 | tf_op jit(solution)/shard_map/all_to_all | solution.py:152
  68.6 3.0 collective-permute-start.3
  72.6 3.0 collective-permute-done.5
  80.2 2.7 collective-permute-start.7
  85.9 3.4 collective-permute-done.8
  92.2 2.7 collective-permute-start.9
  96.1 4.2 all-to-all-start.2
  106.8 6.2 %slice.241 = bf16[16,160,1280]{2,1,0:T(8,128)(2,1)} slice(bf16[16,200,1280]{2,1,0:T(8,128)(2,1)} %bitcast.162), slice={[0:16], [40:200], [0:1280]} | slice | bytes 13107200 | tf_op jit(solution)/shard_map/slice | solution.py:630
  118.3 4.0 all-to-all-done.2
  122.5 8.3 %collective-permute-start.14 = (bf16[2,8,128,256]{3,2,1,0:T(8,128)(2,1)S(1)}, bf16[2,8,128,256]{3,2,1,0:T(8,128)(2,1)S(1)}, u32[]{:S(2)}, u32[]{:S(2)}) collective-permute-start(bf16[2,8,128,256]{3,2,1,0:T(8,128)(2,1)S(1)} %broadcast_select_fusion), channel_id=1, source_target_pairs={{0,2},{2,0},{1,3},{3,1},{4,6},{6,4},{5,7},{7,5},{8,10},{10,8},{9,1... | collective-permute-start | bytes 3145736 | tf_op jit(solution)/shard_map/ppermute | solution.py:51
  133.0 2.7 collective-permute-start.19
  137.0 4.0 collective-permute-done.18
  141.1 6.6 %shard_map.186.attended = bf16[128,1280]{1,0:T(8,128)(2,1)S(1)} custom-call(bf16[128,1280]{1,0:T(8,128)(2,1)S(1)} %multiply_convert_fusion.1, bf16[2,1024,256]{2,1,0:T(8,128)(2,1)S(1)} %bitcast.150, bf16[2,1024,256]{2,1,0:T(8,128)(2,1)S(1)} %bitcast.155, bf16[2,128,256]{2,1,0:T(8,128)(2,1)S(1)} %maximum_select_fusion.refs_2_, ...), custom_call_target="tpu_custom_call" | custom-call | flops 1426063360 | bytes 3997696 | tf_op jit(solution)/shard_map/pallas_call | solution.py:245
  150.0 2.6 collective-permute-start.15
  153.8 25.6 %collective-permute-done.15 = bf16[128,2560]{1,0:T(8,128)(2,1)S(1)} collective-permute-done((bf16[128,2560]{1,0:T(8,128)(2,1)S(1)}, bf16[128,2560]{1,0:T(8,128)(2,1)S(1)}, u32[]{:S(2)}, u32[]{:S(2)}) %collective-permute-start.15) | collective-permute-done | bytes 655392 | tf_op jit(solution)/shard_map/ppermute | solution.py:47
  180.6 2.7 collective-permute-start.20
  183.3 8.0 %collective-permute-done.21 = bf16[128,2560]{1,0:T(8,128)(2,1)S(1)} collective-permute-done((bf16[128,2560]{1,0:T(8,128)(2,1)S(1)}, bf16[128,2560]{1,0:T(8,128)(2,1)S(1)}, u32[]{:S(2)}, u32[]{:S(2)}) %collective-permute-start.21) | collective-permute-done | bytes 655392 | tf_op jit(solution)/shard_map/ppermute | solution.py:43
  191.4 3.1 collective-permute-start.23
  194.6 7.7 %collective-permute-done.22 = bf16[64,2560]{1,0:T(8,128)(2,1)S(1)} collective-permute-done((bf16[64,2560]{1,0:T(8,128)(2,1)S(1)}, bf16[64,2560]{1,0:T(8,128)(2,1)S(1)}, u32[]{:S(2)}, u32[]{:S(2)}) %collective-permute-start.22) | collective-permute-done | bytes 327712 | tf_op jit(solution)/shard_map/ppermute | solution.py:43
  203.9 25.9 %shard_map.187 = (bf16[512,1024]{1,0:T(8,128)(2,1)}, bf16[512,2048]{1,0:T(8,128)(2,1)}, bf16[2560,3072]{1,0:T(8,128)(2,1)}) custom-call(bf16[512,2560]{1,0:T(8,128)(2,1)} %copy-done.53, bf16[512,2560]{1,0:T(8,128)(2,1)} %copy-done.52, bf16[2560,3072]{1,0:T(8,128)(2,1)} %all-gather.5.cloned.1.call-done.gate_weight.up_weight.down_weight, ...), custom_call_target="tpu_custom_call" | custom-call | flops 16106127360 | bytes 39845888 | tf_op jit(solution)/shard_map/pallas_call | solution.py:334
  231.4 8.3 %fusion.4 = bf16[512,2560]{1,0:T(8,128)(2,1)S(1)} fusion(bf16[512,2048]{1,0:T(8,128)(2,1)S(1)} %copy-done.60, bf16[2560,3072]{1,0:T(8,128)(2,1)} %all-gather.5.cloned.1.call-done.gate_weight.up_weight.down_weight), kind=kOutput, calls=%fused_computation.4 | convolution fusion | flops 5370019840 | bytes 15204352 | tf_op jit(solution)/shard_map/tf,ef->te/dot_general | solution.py:662
  239.9 3.2 collective-permute-start.24
  243.5 3.6 collective-permute-done.24
  247.3 3.2 collective-permute-start.25
  250.9 9.4 %collective-permute-done.25 = bf16[128,2560]{1,0:T(8,128)(2,1)S(1)} collective-permute-done((bf16[128,2560]{1,0:T(8,128)(2,1)S(1)}, bf16[128,2560]{1,0:T(8,128)(2,1)S(1)}, u32[]{:S(2)}, u32[]{:S(2)}) %collective-permute-start.25) | collective-permute-done | bytes 655392 | tf_op jit(solution)/shard_map/ppermute | solution.py:43
  260.3 3.6 collective-permute-done.27
  270.5 13.3 %collective-permute-done.28 = bf16[128,2560]{1,0:T(8,128)(2,1)} collective-permute-done((bf16[128,2560]{1,0:T(8,128)(2,1)}, bf16[128,2560]{1,0:T(8,128)(2,1)}, u32[]{:S(2)}, u32[]{:S(2)}) %collective-permute-start.28) | collective-permute-done | bytes 655392 | tf_op jit(solution)/shard_map/ppermute | solution.py:47
  286.0 3.5 fusion.44
  291.3 13.3 %shard_map.188 = (bf16[128,2560]{1,0:T(8,128)(2,1)}, bf16[2,8,2,128,256]{4,3,2,1,0:T(8,128)(2,1)}, bf16[2,128,256]{2,1,0:T(8,128)(2,1)}) custom-call(s32[1]{0:T(128)} %bitcast.36.core, bf16[128,1280]{1,0:T(8,128)(2,1)} %copy-done.27, bf16[128,1280]{1,0:T(8,128)(2,1)} %convolution_convert_fusion.out_grad, bf16[128,1280]{1,0:T(8,128)(2,1)} %copy-done.26, ...), custom_call_target="tpu_custom_call" | custom-call | flops 3565158400 | bytes 6553600 | tf_op jit(solution)/shard_map/pallas_call | solution.py:266
  308.6 21.9 %all-to-all-start.4 = ((bf16[32,128,256]{2,1,0:T(8,128)(2,1)}), bf16[32,128,256]{2,1,0:T(8,128)(2,1)}, u32[]{:S(2)}, u32[]{:S(2)}) async-start(bf16[32,128,256]{2,1,0:T(8,128)(2,1)} %bitcast.175), calls=%async_computation.5 | async-start | bytes 4194304 | tf_op jit(solution)/shard_map/all_to_all | solution.py:684
  333.5 2.6 collective-permute-start.33
  336.1 3.0 collective-permute-start.41
  342.2 4.9 %fusion.2 = f32[512,2560]{1,0:T(8,128)S(1)} fusion(bf16[512,1024]{1,0:T(8,128)(2,1)S(1)} %copy-done.61, bf16[2560,3072]{1,0:T(8,128)(2,1)} %all-gather.5.cloned.1.call-done.gate_weight.up_weight.down_weight), kind=kOutput, calls=%fused_computation.2 | convolution fusion | flops 2684354560 | bytes 11534336 | tf_op jit(solution)/shard_map/tf,ef->te/dot_general | solution.py:679
  350.9 4.5 shard_map.189
  356.7 8.8 %collective-permute-start.39 = (bf16[8,40,2560]{2,1,0:T(8,128)(2,1)}, bf16[8,40,2560]{2,1,0:T(8,128)(2,1)}, u32[]{:S(2)}, u32[]{:S(2)}) collective-permute-start(bf16[8,40,2560]{2,1,0:T(8,128)(2,1)} %dynamic-slice_bitcast_fusion), channel_id=1, source_target_pairs={{0,2},{2,0},{1,3},{3,1},{4,6},{6,4},{5,7},{7,5},{8,10},{10,8},{9,1... | collective-permute-start | bytes 4915208 | tf_op jit(solution)/shard_map/ppermute | solution.py:51
  375.0 2.6 collective-permute-start.44
  377.7 3.1 fusion.9
  380.8 4.6 all-to-all-start.3
  387.2 4.2 collective-permute-done.45.refs_7_
  393.5 3.5 shard_map.190
  399.8 2.7 fusion.17
  403.7 3.3 collective-permute-done.46
  413.0 3.8 collective-permute-start.51
  419.4 5.6 %all-to-all-start.5 = ((bf16[16,40,256]{2,1,0:T(8,128)(2,1)}), bf16[16,40,256]{2,1,0:T(8,128)(2,1)}, u32[]{:S(2)}, u32[]{:S(2)}) async-start(bf16[16,40,256]{2,1,0:T(8,128)(2,1)} %bitcast.84), calls=%async_computation.6 | async-start | bytes 655360 | tf_op jit(solution)/shard_map/all_to_all | solution.py:719
  439.4 6.0 %collective-permute-done.40 = bf16[128,2560]{1,0:T(8,128)(2,1)} collective-permute-done((bf16[128,2560]{1,0:T(8,128)(2,1)}, bf16[128,2560]{1,0:T(8,128)(2,1)}, u32[]{:S(2)}, u32[]{:S(2)}) %collective-permute-start.40) | collective-permute-done | bytes 655392 | tf_op jit(solution)/shard_map/ppermute | solution.py:47
  (370 shorter events, 125.4 us)
Async XLA Ops:
  7.2 82.0 %all-gather.3.cloned.1.call-start = ((), (), s32[]{:S(2)}) async-start(), calls=%async_computation.7 | async-start | bytes 8704000 | tf_op jit(solution)/shard_map/all_gather | solution.py:156
  22.1 180.4 %all-gather.5.cloned.1.call-start = ((), (), s32[]{:S(2)}) async-start(), calls=%async_computation.8 | async-start | bytes 16711680 | tf_op jit(solution)/shard_map/all_gather | solution.py:156
  41.1 15.4 %collective-permute-start = (bf16[128,640]{1,0:T(8,128)(2,1)S(1)}, bf16[128,640]{1,0:T(8,128)(2,1)S(1)}, u32[]{:S(2)}, u32[]{:S(2)}) collective-permute-start(bf16[128,640]{1,0:T(8,128)(2,1)S(1)} %bitcast.183), channel_id=1, source_target_pairs={{0,96},{32,0},{64,32},{96,64},{1,97},{33,1},{65,33},{97,65},{2,98}... | collective-permute-start | bytes 491528 | tf_op jit(solution)/shard_map/ppermute | solution.py:43
  42.1 14.4 %collective-permute-start.1 = (bf16[128,640]{1,0:T(8,128)(2,1)S(1)}, bf16[128,640]{1,0:T(8,128)(2,1)S(1)}, u32[]{:S(2)}, u32[]{:S(2)}) collective-permute-start(bf16[128,640]{1,0:T(8,128)(2,1)S(1)} %bitcast.184), channel_id=1, source_target_pairs={{0,64},{32,96},{64,0},{96,32},{1,65},{33,97},{65,1},{97,33},{2,66}... | collective-permute-start | bytes 491528 | tf_op jit(solution)/shard_map/ppermute | solution.py:43
  43.4 13.1 %collective-permute-start.2 = (bf16[128,640]{1,0:T(8,128)(2,1)S(1)}, bf16[128,640]{1,0:T(8,128)(2,1)S(1)}, u32[]{:S(2)}, u32[]{:S(2)}) collective-permute-start(bf16[128,640]{1,0:T(8,128)(2,1)S(1)} %bitcast.185), channel_id=1, source_target_pairs={{0,32},{32,64},{64,96},{96,0},{1,33},{33,65},{65,97},{97,1},{2,34}... | collective-permute-start | bytes 491528 | tf_op jit(solution)/shard_map/ppermute | solution.py:43
  45.2 23.0 %all-to-all-start.1 = ((bf16[16,40,256]{2,1,0:T(8,128)(2,1)}), bf16[16,40,256]{2,1,0:T(8,128)(2,1)S(1)}, u32[]{:S(2)}, u32[]{:S(2)}) async-start(bf16[16,40,256]{2,1,0:T(8,128)(2,1)} %broadcast_in_dim.118), calls=%async_computation.1 | async-start | bytes 655360 | tf_op jit(solution)/shard_map/all_to_all | solution.py:152
  85.6 9.3 %collective-permute-start.13 = (bf16[128,256]{1,0:T(8,128)(2,1)S(1)}, bf16[128,256]{1,0:T(8,128)(2,1)S(1)}, u32[]{:S(2)}, u32[]{:S(2)}) collective-permute-start(bf16[128,256]{1,0:T(8,128)(2,1)S(1)} %fusion.34), channel_id=1, source_target_pairs={{0,32},{32,64},{64,96},{96,0},{1,33},{33,65},{65,97},{97,1},{2,34}... | collective-permute-start | bytes 196616 | tf_op jit(solution)/shard_map/ppermute | solution.py:43
  96.1 26.2 %all-to-all-start.2 = ((bf16[16,128,256]{2,1,0:T(8,128)(2,1)}), bf16[16,128,256]{2,1,0:T(8,128)(2,1)S(1)}, u32[]{:S(2)}, u32[]{:S(2)}) async-start(bf16[16,128,256]{2,1,0:T(8,128)(2,1)} %bitcast.22), calls=%async_computation.2 | async-start | bytes 2097152 | tf_op jit(solution)/shard_map/all_to_all | solution.py:641
  100.3 307.5 %reduce-scatter.2.cloned.1.call-start = ((), (), s32[]{:S(2)}) async-start(), calls=%async_computation.9 | async-start | bytes 16711680 | tf_op jit(solution)/shard_map/reduce_scatter | solution.py:661
  102.7 10.3 %collective-permute-start.10 = (bf16[128,1280]{1,0:T(8,128)(2,1)}, bf16[128,1280]{1,0:T(8,128)(2,1)}, u32[]{:S(2)}, u32[]{:S(2)}) collective-permute-start(bf16[128,1280]{1,0:T(8,128)(2,1)} %fusion.26), channel_id=1, source_target_pairs={{0,96},{32,0},{64,32},{96,64},{1,97},{33,1},{65,33},{97,65},{2,98}... | collective-permute-start | bytes 983048 | tf_op jit(solution)/shard_map/ppermute | solution.py:43
  103.5 9.6 %collective-permute-start.12 = (bf16[128,1280]{1,0:T(8,128)(2,1)}, bf16[128,1280]{1,0:T(8,128)(2,1)}, u32[]{:S(2)}, u32[]{:S(2)}) collective-permute-start(bf16[128,1280]{1,0:T(8,128)(2,1)} %fusion.27), channel_id=1, source_target_pairs={{0,32},{32,64},{64,96},{96,0},{1,33},{33,65},{65,97},{97,1},{2,34}... | collective-permute-start | bytes 983048 | tf_op jit(solution)/shard_map/ppermute | solution.py:43
  116.8 15.2 %collective-permute-start.16 = (bf16[128,2560]{1,0:T(8,128)(2,1)}, bf16[128,2560]{1,0:T(8,128)(2,1)}, u32[]{:S(2)}, u32[]{:S(2)}) collective-permute-start(bf16[128,2560]{1,0:T(8,128)(2,1)} %copy.68), channel_id=1, source_target_pairs={{0,96},{32,0},{64,32},{96,64},{1,97},{33,1},{65,33},{97,65},{2,98}... | collective-permute-start | bytes 1966088 | tf_op jit(solution)/shard_map/ppermute | solution.py:43
  118.0 12.9 %collective-permute-start.17 = (bf16[128,2560]{1,0:T(8,128)(2,1)}, bf16[128,2560]{1,0:T(8,128)(2,1)}, u32[]{:S(2)}, u32[]{:S(2)}) collective-permute-start(bf16[128,2560]{1,0:T(8,128)(2,1)} %copy.68), channel_id=1, source_target_pairs={{0,32},{32,64},{64,96},{96,0},{1,33},{33,65},{65,97},{97,1},{2,34}... | collective-permute-start | bytes 1966088 | tf_op jit(solution)/shard_map/ppermute | solution.py:43
  122.5 18.6 %collective-permute-start.14 = (bf16[2,8,128,256]{3,2,1,0:T(8,128)(2,1)S(1)}, bf16[2,8,128,256]{3,2,1,0:T(8,128)(2,1)S(1)}, u32[]{:S(2)}, u32[]{:S(2)}) collective-permute-start(bf16[2,8,128,256]{3,2,1,0:T(8,128)(2,1)S(1)} %broadcast_select_fusion), channel_id=1, source_target_pairs={{0,2},{2,0},{1,3},{3,1},{4,6},{6,4},{5,7},{7,5},{8,10},{10,8},{9,1... | collective-permute-start | bytes 3145736 | tf_op jit(solution)/shard_map/ppermute | solution.py:51
  133.0 19.7 %collective-permute-start.19 = (bf16[64,2560]{1,0:T(8,128)(2,1)S(1)}, bf16[64,2560]{1,0:T(8,128)(2,1)S(1)}, u32[]{:S(2)}, u32[]{:S(2)}) collective-permute-start(bf16[64,2560]{1,0:T(8,128)(2,1)S(1)} %slice.246), channel_id=1, source_target_pairs={{0,96},{32,0},{64,32},{96,64},{1,97},{33,1},{65,33},{97,65},{2,98}... | collective-permute-start | bytes 983048 | tf_op jit(solution)/shard_map/ppermute | solution.py:43
  150.0 29.4 %collective-permute-start.15 = (bf16[128,2560]{1,0:T(8,128)(2,1)S(1)}, bf16[128,2560]{1,0:T(8,128)(2,1)S(1)}, u32[]{:S(2)}, u32[]{:S(2)}) collective-permute-start(bf16[128,2560]{1,0:T(8,128)(2,1)S(1)} %fusion.7), channel_id=1, source_target_pairs={{0,1},{1,0},{2,3},{3,2},{4,5},{5,4},{6,7},{7,6},{8,9},{9,8},{10,11... | collective-permute-start | bytes 1966088 | tf_op jit(solution)/shard_map/ppermute | solution.py:47
  180.6 10.6 %collective-permute-start.21 = (bf16[128,2560]{1,0:T(8,128)(2,1)S(1)}, bf16[128,2560]{1,0:T(8,128)(2,1)S(1)}, u32[]{:S(2)}, u32[]{:S(2)}) collective-permute-start(bf16[128,2560]{1,0:T(8,128)(2,1)S(1)} %get-tuple-element.115), channel_id=1, source_target_pairs={{0,32},{32,64},{64,96},{96,0},{1,33},{33,65},{65,97},{97,1},{2,34}... | collective-permute-start | bytes 1966088 | tf_op jit(solution)/shard_map/ppermute | solution.py:43
  180.6 10.8 %collective-permute-start.20 = (bf16[128,2560]{1,0:T(8,128)(2,1)S(1)}, bf16[128,2560]{1,0:T(8,128)(2,1)S(1)}, u32[]{:S(2)}, u32[]{:S(2)}) collective-permute-start(bf16[128,2560]{1,0:T(8,128)(2,1)S(1)} %get-tuple-element.115), channel_id=1, source_target_pairs={{0,96},{32,0},{64,32},{96,64},{1,97},{33,1},{65,33},{97,65},{2,98}... | collective-permute-start | bytes 1966088 | tf_op jit(solution)/shard_map/ppermute | solution.py:43
  191.3 11.0 %collective-permute-start.22 = (bf16[64,2560]{1,0:T(8,128)(2,1)S(1)}, bf16[64,2560]{1,0:T(8,128)(2,1)S(1)}, u32[]{:S(2)}, u32[]{:S(2)}) collective-permute-start(bf16[64,2560]{1,0:T(8,128)(2,1)S(1)} %slice.247), channel_id=1, source_target_pairs={{0,32},{32,64},{64,96},{96,0},{1,33},{33,65},{65,97},{97,1},{2,34}... | collective-permute-start | bytes 983048 | tf_op jit(solution)/shard_map/ppermute | solution.py:43
  191.4 10.9 %collective-permute-start.23 = (bf16[64,2560]{1,0:T(8,128)(2,1)S(1)}, bf16[64,2560]{1,0:T(8,128)(2,1)S(1)}, u32[]{:S(2)}, u32[]{:S(2)}) collective-permute-start(bf16[64,2560]{1,0:T(8,128)(2,1)S(1)} %slice.248), channel_id=1, source_target_pairs={{0,96},{32,0},{64,32},{96,64},{1,97},{33,1},{65,33},{97,65},{2,98}... | collective-permute-start | bytes 983048 | tf_op jit(solution)/shard_map/ppermute | solution.py:43
  247.3 13.0 %collective-permute-start.25 = (bf16[128,2560]{1,0:T(8,128)(2,1)S(1)}, bf16[128,2560]{1,0:T(8,128)(2,1)S(1)}, u32[]{:S(2)}, u32[]{:S(2)}) collective-permute-start(bf16[128,2560]{1,0:T(8,128)(2,1)S(1)} %fusion.18), channel_id=1, source_target_pairs={{0,96},{32,0},{64,32},{96,64},{1,97},{33,1},{65,33},{97,65},{2,98}... | collective-permute-start | bytes 1966088 | tf_op jit(solution)/shard_map/ppermute | solution.py:43
  250.8 13.1 %collective-permute-start.27 = (bf16[128,2560]{1,0:T(8,128)(2,1)S(1)}, bf16[128,2560]{1,0:T(8,128)(2,1)S(1)}, u32[]{:S(2)}, u32[]{:S(2)}) collective-permute-start(bf16[128,2560]{1,0:T(8,128)(2,1)S(1)} %fusion.19), channel_id=1, source_target_pairs={{0,32},{32,64},{64,96},{96,0},{1,33},{33,65},{65,97},{97,1},{2,34}... | collective-permute-start | bytes 1966088 | tf_op jit(solution)/shard_map/ppermute | solution.py:43
  265.0 18.8 %collective-permute-start.28 = (bf16[128,2560]{1,0:T(8,128)(2,1)}, bf16[128,2560]{1,0:T(8,128)(2,1)}, u32[]{:S(2)}, u32[]{:S(2)}) collective-permute-start(bf16[128,2560]{1,0:T(8,128)(2,1)} %reduce-precision_convert_fusion.1), channel_id=1, source_target_pairs={{0,1},{1,0},{2,3},{3,2},{4,5},{5,4},{6,7},{7,6},{8,9},{9,8},{10,11... | collective-permute-start | bytes 1966088 | tf_op jit(solution)/shard_map/ppermute | solution.py:47
  304.6 26.0 %collective-permute-start.29 = (bf16[128,2560]{1,0:T(8,128)(2,1)}, bf16[128,2560]{1,0:T(8,128)(2,1)S(1)}, u32[]{:S(2)}, u32[]{:S(2)}) collective-permute-start(bf16[128,2560]{1,0:T(8,128)(2,1)} %get-tuple-element.65.refs_5_.refs_0_), channel_id=1, source_target_pairs={{0,96},{32,0},{64,32},{96,64},{1,97},{33,1},{65,33},{97,65},{2,98}... | collective-permute-start | bytes 1966088 | tf_op jit(solution)/shard_map/ppermute | solution.py:43
  304.6 26.0 %collective-permute-start.30 = (bf16[128,2560]{1,0:T(8,128)(2,1)}, bf16[128,2560]{1,0:T(8,128)(2,1)S(1)}, u32[]{:S(2)}, u32[]{:S(2)}) collective-permute-start(bf16[128,2560]{1,0:T(8,128)(2,1)} %get-tuple-element.65.refs_5_.refs_0_), channel_id=1, source_target_pairs={{0,64},{32,96},{64,0},{96,32},{1,65},{33,97},{65,1},{97,33},{2,66}... | collective-permute-start | bytes 1966088 | tf_op jit(solution)/shard_map/ppermute | solution.py:43
  305.5 25.1 %collective-permute-start.31 = (bf16[128,2560]{1,0:T(8,128)(2,1)}, bf16[128,2560]{1,0:T(8,128)(2,1)S(1)}, u32[]{:S(2)}, u32[]{:S(2)}) collective-permute-start(bf16[128,2560]{1,0:T(8,128)(2,1)} %get-tuple-element.65.refs_5_.refs_0_), channel_id=1, source_target_pairs={{0,32},{32,64},{64,96},{96,0},{1,33},{33,65},{65,97},{97,1},{2,34}... | collective-permute-start | bytes 1966088 | tf_op jit(solution)/shard_map/ppermute | solution.py:43
  306.1 67.3 %collective-permute-start.42 = (f32[1,128]{1,0:T(1,128)S(1)}, f32[1,128]{1,0:T(1,128)S(1)}, u32[]{:S(2)}, u32[]{:S(2)}) collective-permute-start(f32[1,128]{1,0:T(1,128)S(1)} %bitcast.198), channel_id=1, source_target_pairs={{0,32},{32,64},{64,96},{96,0},{1,33},{33,65},{65,97},{97,1},{2,34}... | collective-permute-start | bytes 1544 | tf_op jit(solution)/shard_map/ppermute | solution.py:43
  308.6 62.2 %all-to-all-start.4 = ((bf16[32,128,256]{2,1,0:T(8,128)(2,1)}), bf16[32,128,256]{2,1,0:T(8,128)(2,1)}, u32[]{:S(2)}, u32[]{:S(2)}) async-start(bf16[32,128,256]{2,1,0:T(8,128)(2,1)} %bitcast.175), calls=%async_computation.5 | async-start | bytes 4194304 | tf_op jit(solution)/shard_map/all_to_all | solution.py:684
  336.1 37.3 %collective-permute-start.41 = (bf16[128,256]{1,0:T(8,128)(2,1)S(1)}, bf16[128,256]{1,0:T(8,128)(2,1)S(1)}, u32[]{:S(2)}, u32[]{:S(2)}) collective-permute-start(bf16[128,256]{1,0:T(8,128)(2,1)S(1)} %select_bitcast_fusion), channel_id=1, source_target_pairs={{0,1},{1,0},{2,3},{3,2},{4,5},{5,4},{6,7},{7,6},{8,9},{9,8},{10,11... | collective-permute-start | bytes 196616 | tf_op jit(solution)/shard_map/ppermute | solution.py:47
  347.2 18.2 %collective-permute-start.35 = (bf16[64,2560]{1,0:T(8,128)(2,1)S(1)}, bf16[64,2560]{1,0:T(8,128)(2,1)S(1)}, u32[]{:S(2)}, u32[]{:S(2)}) collective-permute-start(bf16[64,2560]{1,0:T(8,128)(2,1)S(1)} %get-tuple-element.146), channel_id=1, source_target_pairs={{0,96},{32,0},{64,32},{96,64},{1,97},{33,1},{65,33},{97,65},{2,98}... | collective-permute-start | bytes 983048 | tf_op jit(solution)/shard_map/ppermute | solution.py:43
  348.1 17.4 %collective-permute-start.37 = (bf16[64,2560]{1,0:T(8,128)(2,1)S(1)}, bf16[64,2560]{1,0:T(8,128)(2,1)S(1)}, u32[]{:S(2)}, u32[]{:S(2)}) collective-permute-start(bf16[64,2560]{1,0:T(8,128)(2,1)S(1)} %get-tuple-element.147), channel_id=1, source_target_pairs={{0,32},{32,64},{64,96},{96,0},{1,33},{33,65},{65,97},{97,1},{2,34}... | collective-permute-start | bytes 983048 | tf_op jit(solution)/shard_map/ppermute | solution.py:43
  356.7 21.0 %collective-permute-start.39 = (bf16[8,40,2560]{2,1,0:T(8,128)(2,1)}, bf16[8,40,2560]{2,1,0:T(8,128)(2,1)}, u32[]{:S(2)}, u32[]{:S(2)}) collective-permute-start(bf16[8,40,2560]{2,1,0:T(8,128)(2,1)} %dynamic-slice_bitcast_fusion), channel_id=1, source_target_pairs={{0,2},{2,0},{1,3},{3,1},{4,6},{6,4},{5,7},{7,5},{8,10},{10,8},{9,1... | collective-permute-start | bytes 4915208 | tf_op jit(solution)/shard_map/ppermute | solution.py:51
  366.7 33.1 %collective-permute-start.36 = (bf16[128,2560]{1,0:T(8,128)(2,1)}, bf16[128,2560]{1,0:T(8,128)(2,1)}, u32[]{:S(2)}, u32[]{:S(2)}) collective-permute-start(bf16[128,2560]{1,0:T(8,128)(2,1)} %fusion.20), channel_id=1, source_target_pairs={{0,96},{32,0},{64,32},{96,64},{1,97},{33,1},{65,33},{97,65},{2,98}... | collective-permute-start | bytes 1966088 | tf_op jit(solution)/shard_map/ppermute | solution.py:43
  368.2 31.6 %collective-permute-start.38 = (bf16[128,2560]{1,0:T(8,128)(2,1)}, bf16[128,2560]{1,0:T(8,128)(2,1)}, u32[]{:S(2)}, u32[]{:S(2)}) collective-permute-start(bf16[128,2560]{1,0:T(8,128)(2,1)} %fusion.21), channel_id=1, source_target_pairs={{0,32},{32,64},{64,96},{96,0},{1,33},{33,65},{65,97},{97,1},{2,34}... | collective-permute-start | bytes 1966088 | tf_op jit(solution)/shard_map/ppermute | solution.py:43
  373.5 12.6 %collective-permute-start.43 = (bf16[256,256]{1,0:T(8,128)(2,1)S(1)}, bf16[256,256]{1,0:T(8,128)(2,1)S(1)}, u32[]{:S(2)}, u32[]{:S(2)}) collective-permute-start(bf16[256,256]{1,0:T(8,128)(2,1)S(1)} %fusion.28.refs_4_), channel_id=1, source_target_pairs={{0,96},{32,0},{64,32},{96,64},{1,97},{33,1},{65,33},{97,65},{2,98}... | collective-permute-start | bytes 393224 | tf_op jit(solution)/shard_map/ppermute | solution.py:43
  375.0 12.2 %collective-permute-start.44 = (bf16[256,256]{1,0:T(8,128)(2,1)S(1)}, bf16[256,256]{1,0:T(8,128)(2,1)}, u32[]{:S(2)}, u32[]{:S(2)}) collective-permute-start(bf16[256,256]{1,0:T(8,128)(2,1)S(1)} %fusion.28.refs_4_), channel_id=1, source_target_pairs={{0,64},{32,96},{64,0},{96,32},{1,65},{33,97},{65,1},{97,33},{2,66}... | collective-permute-start | bytes 393224 | tf_op jit(solution)/shard_map/ppermute | solution.py:43
  377.7 13.7 %collective-permute-start.45 = (bf16[256,256]{1,0:T(8,128)(2,1)S(1)}, bf16[256,256]{1,0:T(8,128)(2,1)}, u32[]{:S(2)}, u32[]{:S(2)}) collective-permute-start(bf16[256,256]{1,0:T(8,128)(2,1)S(1)} %fusion.28.refs_4_), channel_id=1, source_target_pairs={{0,32},{32,64},{64,96},{96,0},{1,33},{33,65},{65,97},{97,1},{2,34}... | collective-permute-start | bytes 393224 | tf_op jit(solution)/shard_map/ppermute | solution.py:43
  380.8 27.1 %all-to-all-start.3 = ((bf16[8,40,2560]{2,1,0:T(8,128)(2,1)}), bf16[8,40,2560]{2,1,0:T(8,128)(2,1)}, u32[]{:S(2)}, u32[]{:S(2)}) async-start(bf16[8,40,2560]{2,1,0:T(8,128)(2,1)} %fusion.9), calls=%async_computation.4 | async-start | bytes 3276800 | tf_op jit(solution)/shard_map/all_to_all | solution.py:706
  397.0 9.9 %collective-permute-start.46 = (bf16[128,640]{1,0:T(8,128)(2,1)S(1)}, bf16[128,640]{1,0:T(8,128)(2,1)S(1)}, u32[]{:S(2)}, u32[]{:S(2)}) collective-permute-start(bf16[128,640]{1,0:T(8,128)(2,1)S(1)} %get-tuple-element.73), channel_id=1, source_target_pairs={{0,32},{32,64},{64,96},{96,0},{1,33},{33,65},{65,97},{97,1},{2,34}... | collective-permute-start | bytes 491528 | tf_op jit(solution)/shard_map/ppermute | solution.py:43
  397.1 9.8 %collective-permute-start.47 = (bf16[128,640]{1,0:T(8,128)(2,1)S(1)}, bf16[128,640]{1,0:T(8,128)(2,1)S(1)}, u32[]{:S(2)}, u32[]{:S(2)}) collective-permute-start(bf16[128,640]{1,0:T(8,128)(2,1)S(1)} %get-tuple-element.74), channel_id=1, source_target_pairs={{0,64},{32,96},{64,0},{96,32},{1,65},{33,97},{65,1},{97,33},{2,66}... | collective-permute-start | bytes 491528 | tf_op jit(solution)/shard_map/ppermute | solution.py:43
  407.9 27.0 %collective-permute-start.49 = (bf16[128,2560]{0,1:T(8,128)(2,1)S(1)}, bf16[128,2560]{0,1:T(8,128)(2,1)}, u32[]{:S(2)}, u32[]{:S(2)}) collective-permute-start(bf16[128,2560]{0,1:T(8,128)(2,1)S(1)} %reduce-precision_convert_fusion), channel_id=1, source_target_pairs={{0,1},{1,0},{2,3},{3,2},{4,5},{5,4},{6,7},{7,6},{8,9},{9,8},{10,11... | collective-permute-start | bytes 1966088 | tf_op jit(solution)/shard_map/ppermute | solution.py:47
  412.2 16.8 %collective-permute-start.50 = (bf16[40,3072]{1,0:T(8,128)(2,1)}, bf16[40,3072]{1,0:T(8,128)(2,1)}, u32[]{:S(2)}, u32[]{:S(2)}) collective-permute-start(bf16[40,3072]{1,0:T(8,128)(2,1)} %get-tuple-element.141), channel_id=1, source_target_pairs={{0,32},{32,64},{64,96},{96,0},{1,33},{33,65},{65,97},{97,1},{2,34}... | collective-permute-start | bytes 737288 | tf_op jit(solution)/shard_map/ppermute | solution.py:43
  413.0 16.0 %collective-permute-start.51 = (bf16[40,3072]{1,0:T(8,128)(2,1)}, bf16[40,3072]{1,0:T(8,128)(2,1)}, u32[]{:S(2)}, u32[]{:S(2)}) collective-permute-start(bf16[40,3072]{1,0:T(8,128)(2,1)} %get-tuple-element.140), channel_id=1, source_target_pairs={{0,64},{32,96},{64,0},{96,32},{1,65},{33,97},{65,1},{97,33},{2,66}... | collective-permute-start | bytes 737288 | tf_op jit(solution)/shard_map/ppermute | solution.py:43
  416.8 12.2 %collective-permute-start.52 = (bf16[40,3072]{1,0:T(8,128)(2,1)}, bf16[40,3072]{1,0:T(8,128)(2,1)}, u32[]{:S(2)}, u32[]{:S(2)}) collective-permute-start(bf16[40,3072]{1,0:T(8,128)(2,1)} %get-tuple-element.139), channel_id=1, source_target_pairs={{0,96},{32,0},{64,32},{96,64},{1,97},{33,1},{65,33},{97,65},{2,98}... | collective-permute-start | bytes 737288 | tf_op jit(solution)/shard_map/ppermute | solution.py:43
  419.4 14.3 %all-to-all-start.5 = ((bf16[16,40,256]{2,1,0:T(8,128)(2,1)}), bf16[16,40,256]{2,1,0:T(8,128)(2,1)}, u32[]{:S(2)}, u32[]{:S(2)}) async-start(bf16[16,40,256]{2,1,0:T(8,128)(2,1)} %bitcast.84), calls=%async_computation.6 | async-start | bytes 655360 | tf_op jit(solution)/shard_map/all_to_all | solution.py:719
  426.6 18.8 %collective-permute-start.40 = (bf16[128,2560]{1,0:T(8,128)(2,1)}, bf16[128,2560]{1,0:T(8,128)(2,1)}, u32[]{:S(2)}, u32[]{:S(2)}) collective-permute-start(bf16[128,2560]{1,0:T(8,128)(2,1)} %fusion.17), channel_id=1, source_target_pairs={{0,1},{1,0},{2,3},{3,2},{4,5},{5,4},{6,7},{7,6},{8,9},{9,8},{10,11... | collective-permute-start | bytes 1966088 | tf_op jit(solution)/shard_map/ppermute | solution.py:47
  434.9 17.5 %collective-permute-start.53 = (f32[2,40]{1,0:T(2,128)S(1)}, f32[2,40]{1,0:T(2,128)S(1)}, u32[]{:S(2)}, u32[]{:S(2)}) collective-permute-start(f32[2,40]{1,0:T(2,128)S(1)} %pad_maximum_fusion.6), channel_id=1, source_target_pairs={{0,1},{1,0},{2,3},{3,2},{4,5},{5,4},{6,7},{7,6},{8,9},{9,8},{10,11... | collective-permute-start | bytes 968 | tf_op jit(solution)/shard_map/ppermute | solution.py:47
  436.4 16.6 %collective-permute-start.54 = (f32[40,256]{1,0:T(8,128)S(1)}, f32[40,256]{1,0:T(8,128)S(1)}, u32[]{:S(2)}, u32[]{:S(2)}) collective-permute-start(f32[40,256]{1,0:T(8,128)S(1)} %convert_reduce_fusion.3), channel_id=1, source_target_pairs={{0,1},{1,0},{2,3},{3,2},{4,5},{5,4},{6,7},{7,6},{8,9},{9,8},{10,11... | collective-permute-start | bytes 122888 | tf_op jit(solution)/shard_map/ppermute | solution.py:47
  (79 other events, 890.5 us)
Sparse Core Ops, SparseCore 0:
  22.2 59.1 all-gather.2
  83.1 112.9 all-gather.4
  230.0 139.5 reduce-scatter.1

commit v2 on v1

--- a/solution.py
+++ b/solution.py
@@ -738,9 +738,12 @@
         * jnp.mean(weighted_one * tokens_in, axis=-1, keepdims=True)
     )
 
-    ffn_sum = ffn_low.astype(F32) + swap(ffn_low).astype(F32)
-    activations = restore_features((middle + ffn_sum).astype(BF16))
+    ffn_low = restore_features(ffn_low)
+    ffn_other = swap(ffn_low)
+    ffn_sum = ffn_low.astype(F32) + ffn_other.astype(F32)
+    activations = (restore_features(middle) + ffn_sum).astype(BF16)
     ffn_grad_own = exchange_planes(ffn_grad_rows.reshape(PLANES, own, 3 * padded))
+    ffn_grad_own[0] = after(ffn_grad_own[0], ffn_other)
     gate_weight_grad, up_weight_grad, down_rows, ffn_gain_part = join(
         ffn_grad_own, gate_weight, up_weight, gain_two
     )

time: 471 us -> 476 us (1.011)
  the two profiles are of different devices: /device:TPU:1 before, /device:TPU:14 now
where the time goes in v2:
time: 476 us; the launch traced here: 467 us
  waiting for transfers between devices  139 us (29%)
  starting transfers between devices  119 us (25%)
  Pallas kernels  57.2 us (12%)
  local copies, waits for them, and re-layouts  49.7 us (10%)
  other arithmetic  39.1 us (8%)
  blocking collectives  27.8 us (6%)
  matrix products  19 us (4%)
  between operations  15.9 us (3%)
    ppermute x45, starting transfers between devices, to_plane(): lax.ppermute(block, X, [(i, (i + shift) % PLANES) for i in range(PLANES)])  72 us
    ppermute x45, waiting for transfers between devices, to_plane(): lax.ppermute(block, X, [(i, (i + shift) % PLANES) for i in range(PLANES)])  61.5 us
    ppermute x8, waiting for transfers between devices, swap(): return lax.ppermute(block, M, [(0, 1), (1, 0)])  44.4 us
    pallas_call x1, Pallas kernels, geglu(): pl.pallas_call(functools.partial(geglu_kernel, steps), grid=(steps + PLAN...  25.8 us
    ppermute x8, starting transfers between devices, swap(): return lax.ppermute(block, M, [(0, 1), (1, 0)])  16.3 us
    all_to_all x1, waiting for transfers between devices, body(): lax.all_to_all(after(token_outer((inputs_cut, keyval_all)), attn_met), R,...  15 us
    all_to_all x1, blocking collectives, body(): ffn_own = lax.all_to_all(after(ffn_own, out_planes), X, 0, 0, tiled=True)  14.4 us
    pallas_call x1, Pallas kernels, attend_back(): pl.pallas_call(attend_back_kernel, grid=(heads,), in_specs=[pl.BlockSpec(...  13.4 us
  transfers between devices with their start and end apart: 63, of which 26 were waited for; matrix products, arithmetic and copies ran while one was open for 21% of the time, Pallas kernels for 7%

profile of v2, /device:TPU:14, one launch (start us, length us, event | category | flops | bytes accessed | tf_op | source)
XLA Modules:
  0.0 466.9 jit_solution(13089486363965756361)
XLA Ops:
  7.3 13.4 %all_gather.9 = bf16[160,1280]{1,0:T(8,128)(2,1)S(1)} all-gather(bf16[40,1280]{1,0:T(8,128)(2,1)} %bitcast.194), channel_id=1, replica_groups=mesh['x'=4,'yl'=2,'z'=4,'c'=2,'mp'=2] {'x'}, dimensions={0}, use_global_device_ids=true | all-gather | bytes 512000 | tf_op jit(solution)/shard_map/all_gather | solution.py:563
  26.5 14.4 %all_to_all.56 = bf16[4,40,3072]{2,1,0:T(8,128)(2,1)} all-to-all(bf16[4,40,3072]{2,1,0:T(8,128)(2,1)S(1)} %copy.58), channel_id=1, replica_groups=mesh['x'=4,'yl'=2,'z'=4,'c'=2,'mp'=2] {'x'}, dimensions={0} | all-to-all | bytes 1966080 | tf_op jit(solution)/shard_map/all_to_all | solution.py:565
  43.1 3.2 collective-permute-start.1
  49.4 6.8 %all-to-all-start.1 = ((bf16[16,40,256]{2,1,0:T(8,128)(2,1)}), bf16[16,40,256]{2,1,0:T(8,128)(2,1)S(1)}, u32[]{:S(2)}, u32[]{:S(2)}) async-start(bf16[16,40,256]{2,1,0:T(8,128)(2,1)} %broadcast_in_dim.118), calls=%async_computation.1 | async-start | bytes 655360 | tf_op jit(solution)/shard_map/all_to_all | solution.py:152
  58.2 9.2 %all-to-all-done.1 = bf16[16,40,256]{2,1,0:T(8,128)(2,1)S(1)} async-done(((bf16[16,40,256]{2,1,0:T(8,128)(2,1)}), bf16[16,40,256]{2,1,0:T(8,128)(2,1)S(1)}, u32[]{:S(2)}, u32[]{:S(2)}) %all-to-all-start.1) | async-done | bytes 327712 | tf_op jit(solution)/shard_map/all_to_all | solution.py:152
  73.3 3.1 collective-permute-start.6
  81.5 3.0 collective-permute-done.7
  84.5 3.3 collective-permute-start.8
  92.7 3.6 collective-permute-start.11
  97.5 5.7 %all-to-all-start.2 = ((bf16[16,128,256]{2,1,0:T(8,128)(2,1)}), bf16[16,128,256]{2,1,0:T(8,128)(2,1)S(1)}, u32[]{:S(2)}, u32[]{:S(2)}) async-start(bf16[16,128,256]{2,1,0:T(8,128)(2,1)} %bitcast.22), calls=%async_computation.2 | async-start | bytes 2097152 | tf_op jit(solution)/shard_map/all_to_all | solution.py:641
  105.5 3.3 collective-permute-start.12
  108.9 2.6 copy.63
  111.5 6.0 %slice.241 = bf16[16,160,1280]{2,1,0:T(8,128)(2,1)} slice(bf16[16,200,1280]{2,1,0:T(8,128)(2,1)} %bitcast.170), slice={[0:16], [40:200], [0:1280]} | slice | bytes 13107200 | tf_op jit(solution)/shard_map/slice | solution.py:630
  119.9 3.2 collective-permute-start.17
  125.1 7.9 %collective-permute-done.17 = bf16[128,2560]{1,0:T(8,128)(2,1)} collective-permute-done((bf16[128,2560]{1,0:T(8,128)(2,1)}, bf16[128,2560]{1,0:T(8,128)(2,1)}, u32[]{:S(2)}, u32[]{:S(2)}) %collective-permute-start.17) | collective-permute-done | bytes 655392 | tf_op jit(solution)/shard_map/ppermute | solution.py:43
  134.0 3.8 collective-permute-start.18
  142.5 6.6 %shard_map.186.attended = bf16[128,1280]{1,0:T(8,128)(2,1)S(1)} custom-call(bf16[128,1280]{1,0:T(8,128)(2,1)S(1)} %multiply_convert_fusion.1, bf16[2,1024,256]{2,1,0:T(8,128)(2,1)S(1)} %bitcast.158, bf16[2,1024,256]{2,1,0:T(8,128)(2,1)S(1)} %bitcast.163, bf16[2,128,256]{2,1,0:T(8,128)(2,1)S(1)} %maximum_select_fusion.refs_2_, ...), custom_call_target="tpu_custom_call" | custom-call | flops 1426063360 | bytes 3997696 | tf_op jit(solution)/shard_map/pallas_call | solution.py:245
  154.9 26.9 %collective-permute-done.15 = bf16[128,2560]{1,0:T(8,128)(2,1)S(1)} collective-permute-done((bf16[128,2560]{1,0:T(8,128)(2,1)S(1)}, bf16[128,2560]{1,0:T(8,128)(2,1)S(1)}, u32[]{:S(2)}, u32[]{:S(2)}) %collective-permute-start.15) | collective-permute-done | bytes 655392 | tf_op jit(solution)/shard_map/ppermute | solution.py:47
  183.4 3.6 collective-permute-start.21
  187.0 11.6 %collective-permute-done.21 = bf16[128,2560]{1,0:T(8,128)(2,1)S(1)} collective-permute-done((bf16[128,2560]{1,0:T(8,128)(2,1)S(1)}, bf16[128,2560]{1,0:T(8,128)(2,1)S(1)}, u32[]{:S(2)}, u32[]{:S(2)}) %collective-permute-start.21) | collective-permute-done | bytes 655392 | tf_op jit(solution)/shard_map/ppermute | solution.py:43
  198.6 3.8 collective-permute-start.22
  202.9 4.0 collective-permute-done.22
  207.0 4.2 collective-permute-done.23
  212.8 25.8 %shard_map.187 = (bf16[512,1024]{1,0:T(8,128)(2,1)}, bf16[512,2048]{1,0:T(8,128)(2,1)}, bf16[2560,3072]{1,0:T(8,128)(2,1)}) custom-call(bf16[512,2560]{1,0:T(8,128)(2,1)} %copy-done.56, bf16[512,2560]{1,0:T(8,128)(2,1)} %copy-done.55, bf16[2560,3072]{1,0:T(8,128)(2,1)} %all-gather.5.cloned.1.call-done.gate_weight.up_weight.down_weight, ...), custom_call_target="tpu_custom_call" | custom-call | flops 16106127360 | bytes 39845888 | tf_op jit(solution)/shard_map/pallas_call | solution.py:334
  240.2 8.5 %fusion.4 = bf16[512,2560]{1,0:T(8,128)(2,1)S(1)} fusion(bf16[512,2048]{1,0:T(8,128)(2,1)S(1)} %copy-done.63, bf16[2560,3072]{1,0:T(8,128)(2,1)} %all-gather.5.cloned.1.call-done.gate_weight.up_weight.down_weight), kind=kOutput, calls=%fused_computation.4 | convolution fusion | flops 5370019840 | bytes 15204352 | tf_op jit(solution)/shard_map/tf,ef->te/dot_general | solution.py:662
  249.2 3.3 collective-permute-start.26
  252.5 7.5 %collective-permute-done.24 = bf16[64,2560]{1,0:T(8,128)(2,1)S(1)} collective-permute-done((bf16[64,2560]{1,0:T(8,128)(2,1)S(1)}, bf16[64,2560]{1,0:T(8,128)(2,1)S(1)}, u32[]{:S(2)}, u32[]{:S(2)}) %collective-permute-start.24) | collective-permute-done | bytes 327712 | tf_op jit(solution)/shard_map/ppermute | solution.py:43
  260.4 3.3 collective-permute-start.27
  263.7 8.3 %collective-permute-done.25 = bf16[128,2560]{1,0:T(8,128)(2,1)S(1)} collective-permute-done((bf16[128,2560]{1,0:T(8,128)(2,1)S(1)}, bf16[128,2560]{1,0:T(8,128)(2,1)S(1)}, u32[]{:S(2)}, u32[]{:S(2)}) %collective-permute-start.25) | collective-permute-done | bytes 655392 | tf_op jit(solution)/shard_map/ppermute | solution.py:43
  277.5 14.5 %collective-permute-done.28 = bf16[128,2560]{1,0:T(8,128)(2,1)} collective-permute-done((bf16[128,2560]{1,0:T(8,128)(2,1)S(1)}, bf16[128,2560]{1,0:T(8,128)(2,1)}, u32[]{:S(2)}, u32[]{:S(2)}) %collective-permute-start.28) | collective-permute-done | bytes 655392 | tf_op jit(solution)/shard_map/ppermute | solution.py:47
  293.8 3.3 fusion.45
  298.9 13.4 %shard_map.188 = (bf16[128,2560]{1,0:T(8,128)(2,1)}, bf16[2,8,2,128,256]{4,3,2,1,0:T(8,128)(2,1)}, bf16[2,128,256]{2,1,0:T(8,128)(2,1)}) custom-call(s32[1]{0:T(128)} %bitcast.39.core, bf16[128,1280]{1,0:T(8,128)(2,1)} %copy-done.27, bf16[128,1280]{1,0:T(8,128)(2,1)} %convolution_convert_fusion.out_grad, bf16[128,1280]{1,0:T(8,128)(2,1)} %copy-done.26, ...), custom_call_target="tpu_custom_call" | custom-call | flops 3565158400 | bytes 6553600 | tf_op jit(solution)/shard_map/pallas_call | solution.py:266
  312.4 4.7 %collective-permute-start.30 = (bf16[128,2560]{1,0:T(8,128)(2,1)}, bf16[128,2560]{1,0:T(8,128)(2,1)S(1)}, u32[]{:S(2)}, u32[]{:S(2)}) collective-permute-start(bf16[128,2560]{1,0:T(8,128)(2,1)} %get-tuple-element.66.refs_5_.refs_0_), channel_id=1, source_target_pairs={{0,64},{32,96},{64,0},{96,32},{1,65},{33,97},{65,1},{97,33},{2,66}... | collective-permute-start | bytes 1966088 | tf_op jit(solution)/shard_map/ppermute | solution.py:43
  320.4 2.5 copy.73
  322.9 7.7 %all-to-all-start.4 = ((bf16[32,128,256]{2,1,0:T(8,128)(2,1)}), bf16[32,128,256]{2,1,0:T(8,128)(2,1)}, u32[]{:S(2)}, u32[]{:S(2)}) async-start(bf16[32,128,256]{2,1,0:T(8,128)(2,1)} %bitcast.183), calls=%async_computation.5 | async-start | bytes 4194304 | tf_op jit(solution)/shard_map/all_to_all | solution.py:684
  334.3 3.1 collective-permute-start.33
  343.7 5.0 %fusion.2 = f32[512,2560]{1,0:T(8,128)S(1)} fusion(bf16[512,1024]{1,0:T(8,128)(2,1)S(1)} %copy-done.64, bf16[2560,3072]{1,0:T(8,128)(2,1)} %all-gather.5.cloned.1.call-done.gate_weight.up_weight.down_weight), kind=kOutput, calls=%fused_computation.2 | convolution fusion | flops 2684354560 | bytes 11534336 | tf_op jit(solution)/shard_map/tf,ef->te/dot_general | solution.py:679
  352.5 4.5 shard_map.189
  364.7 5.7 %all-to-all-done.4 = bf16[32,128,256]{2,1,0:T(8,128)(2,1)} async-done(((bf16[32,128,256]{2,1,0:T(8,128)(2,1)}), bf16[32,128,256]{2,1,0:T(8,128)(2,1)}, u32[]{:S(2)}, u32[]{:S(2)}) %all-to-all-start.4) | async-done | bytes 2097184 | tf_op jit(solution)/shard_map/all_to_all | solution.py:684
  377.3 3.0 fusion.9
  380.3 5.6 %all-to-all-start.3 = ((bf16[8,40,2560]{2,1,0:T(8,128)(2,1)}), bf16[8,40,2560]{2,1,0:T(8,128)(2,1)}, u32[]{:S(2)}, u32[]{:S(2)}) async-start(bf16[8,40,2560]{2,1,0:T(8,128)(2,1)} %fusion.9), calls=%async_computation.4 | async-start | bytes 3276800 | tf_op jit(solution)/shard_map/all_to_all | solution.py:706
  388.1 3.5 shard_map.190
  398.1 2.8 collective-permute-done.47
  413.4 2.8 collective-permute-start.40
  416.2 2.5 convert_reduce_fusion.2
  418.7 4.9 %all-to-all-start.5 = ((bf16[16,40,256]{2,1,0:T(8,128)(2,1)}), bf16[16,40,256]{2,1,0:T(8,128)(2,1)}, u32[]{:S(2)}, u32[]{:S(2)}) async-start(bf16[16,40,256]{2,1,0:T(8,128)(2,1)} %bitcast.87), calls=%async_computation.6 | async-start | bytes 655360 | tf_op jit(solution)/shard_map/all_to_all | solution.py:719
  427.6 15.0 %all-to-all-done.5 = bf16[16,40,256]{2,1,0:T(8,128)(2,1)} async-done(((bf16[16,40,256]{2,1,0:T(8,128)(2,1)}), bf16[16,40,256]{2,1,0:T(8,128)(2,1)}, u32[]{:S(2)}, u32[]{:S(2)}) %all-to-all-start.5) | async-done | bytes 327712 | tf_op jit(solution)/shard_map/all_to_all | solution.py:719
  451.0 2.7 fusion.12
  (378 shorter events, 133.9 us)
Async XLA Ops:
  7.2 82.5 %all-gather.3.cloned.1.call-start = ((), (), s32[]{:S(2)}) async-start(), calls=%async_computation.7 | async-start | bytes 8704000 | tf_op jit(solution)/shard_map/all_gather | solution.py:156
  23.1 188.1 %all-gather.5.cloned.1.call-start = ((), (), s32[]{:S(2)}) async-start(), calls=%async_computation.8 | async-start | bytes 16711680 | tf_op jit(solution)/shard_map/all_gather | solution.py:156
  42.6 13.6 %collective-permute-start = (bf16[128,640]{1,0:T(8,128)(2,1)S(1)}, bf16[128,640]{1,0:T(8,128)(2,1)S(1)}, u32[]{:S(2)}, u32[]{:S(2)}) collective-permute-start(bf16[128,640]{1,0:T(8,128)(2,1)S(1)} %bitcast.191), channel_id=1, source_target_pairs={{0,96},{32,0},{64,32},{96,64},{1,97},{33,1},{65,33},{97,65},{2,98}... | collective-permute-start | bytes 491528 | tf_op jit(solution)/shard_map/ppermute | solution.py:43
  43.1 13.1 %collective-permute-start.1 = (bf16[128,640]{1,0:T(8,128)(2,1)S(1)}, bf16[128,640]{1,0:T(8,128)(2,1)S(1)}, u32[]{:S(2)}, u32[]{:S(2)}) collective-permute-start(bf16[128,640]{1,0:T(8,128)(2,1)S(1)} %bitcast.192), channel_id=1, source_target_pairs={{0,64},{32,96},{64,0},{96,32},{1,65},{33,97},{65,1},{97,33},{2,66}... | collective-permute-start | bytes 491528 | tf_op jit(solution)/shard_map/ppermute | solution.py:43
  46.3 9.9 %collective-permute-start.2 = (bf16[128,640]{1,0:T(8,128)(2,1)S(1)}, bf16[128,640]{1,0:T(8,128)(2,1)S(1)}, u32[]{:S(2)}, u32[]{:S(2)}) collective-permute-start(bf16[128,640]{1,0:T(8,128)(2,1)S(1)} %bitcast.193), channel_id=1, source_target_pairs={{0,32},{32,64},{64,96},{96,0},{1,33},{33,65},{65,97},{97,1},{2,34}... | collective-permute-start | bytes 491528 | tf_op jit(solution)/shard_map/ppermute | solution.py:43
  49.4 18.0 %all-to-all-start.1 = ((bf16[16,40,256]{2,1,0:T(8,128)(2,1)}), bf16[16,40,256]{2,1,0:T(8,128)(2,1)S(1)}, u32[]{:S(2)}, u32[]{:S(2)}) async-start(bf16[16,40,256]{2,1,0:T(8,128)(2,1)} %broadcast_in_dim.118), calls=%async_computation.1 | async-start | bytes 655360 | tf_op jit(solution)/shard_map/all_to_all | solution.py:152
  92.7 10.6 %collective-permute-start.11 = (bf16[64,1280]{1,0:T(8,128)(2,1)S(1)}, bf16[64,1280]{1,0:T(8,128)(2,1)S(1)}, u32[]{:S(2)}, u32[]{:S(2)}) collective-permute-start(bf16[64,1280]{1,0:T(8,128)(2,1)S(1)} %get-tuple-element.170), channel_id=1, source_target_pairs={{0,32},{32,64},{64,96},{96,0},{1,33},{33,65},{65,97},{97,1},{2,34}... | collective-permute-start | bytes 491528 | tf_op jit(solution)/shard_map/ppermute | solution.py:43
  97.5 27.3 %all-to-all-start.2 = ((bf16[16,128,256]{2,1,0:T(8,128)(2,1)}), bf16[16,128,256]{2,1,0:T(8,128)(2,1)S(1)}, u32[]{:S(2)}, u32[]{:S(2)}) async-start(bf16[16,128,256]{2,1,0:T(8,128)(2,1)} %bitcast.22), calls=%async_computation.2 | async-start | bytes 2097152 | tf_op jit(solution)/shard_map/all_to_all | solution.py:641
  103.2 302.7 %reduce-scatter.2.cloned.1.call-start = ((), (), s32[]{:S(2)}) async-start(), calls=%async_computation.9 | async-start | bytes 16711680 | tf_op jit(solution)/shard_map/reduce_scatter | solution.py:661
  105.4 12.0 %collective-permute-start.10 = (bf16[128,1280]{1,0:T(8,128)(2,1)}, bf16[128,1280]{1,0:T(8,128)(2,1)S(1)}, u32[]{:S(2)}, u32[]{:S(2)}) collective-permute-start(bf16[128,1280]{1,0:T(8,128)(2,1)} %fusion.27), channel_id=1, source_target_pairs={{0,96},{32,0},{64,32},{96,64},{1,97},{33,1},{65,33},{97,65},{2,98}... | collective-permute-start | bytes 983048 | tf_op jit(solution)/shard_map/ppermute | solution.py:43
  105.5 12.0 %collective-permute-start.12 = (bf16[128,1280]{1,0:T(8,128)(2,1)S(1)}, bf16[128,1280]{1,0:T(8,128)(2,1)}, u32[]{:S(2)}, u32[]{:S(2)}) collective-permute-start(bf16[128,1280]{1,0:T(8,128)(2,1)S(1)} %fusion.28), channel_id=1, source_target_pairs={{0,32},{32,64},{64,96},{96,0},{1,33},{33,65},{65,97},{97,1},{2,34}... | collective-permute-start | bytes 983048 | tf_op jit(solution)/shard_map/ppermute | solution.py:43
  119.9 17.9 %collective-permute-start.16 = (bf16[128,2560]{1,0:T(8,128)(2,1)}, bf16[128,2560]{1,0:T(8,128)(2,1)}, u32[]{:S(2)}, u32[]{:S(2)}) collective-permute-start(bf16[128,2560]{1,0:T(8,128)(2,1)} %copy.71), channel_id=1, source_target_pairs={{0,96},{32,0},{64,32},{96,64},{1,97},{33,1},{65,33},{97,65},{2,98}... | collective-permute-start | bytes 1966088 | tf_op jit(solution)/shard_map/ppermute | solution.py:43
  119.9 13.1 %collective-permute-start.17 = (bf16[128,2560]{1,0:T(8,128)(2,1)}, bf16[128,2560]{1,0:T(8,128)(2,1)}, u32[]{:S(2)}, u32[]{:S(2)}) collective-permute-start(bf16[128,2560]{1,0:T(8,128)(2,1)} %copy.71), channel_id=1, source_target_pairs={{0,32},{32,64},{64,96},{96,0},{1,33},{33,65},{65,97},{97,1},{2,34}... | collective-permute-start | bytes 1966088 | tf_op jit(solution)/shard_map/ppermute | solution.py:43
  125.0 17.4 %collective-permute-start.14 = (bf16[2,8,128,256]{3,2,1,0:T(8,128)(2,1)S(1)}, bf16[2,8,128,256]{3,2,1,0:T(8,128)(2,1)S(1)}, u32[]{:S(2)}, u32[]{:S(2)}) collective-permute-start(bf16[2,8,128,256]{3,2,1,0:T(8,128)(2,1)S(1)} %broadcast_select_fusion), channel_id=1, source_target_pairs={{0,2},{2,0},{1,3},{3,1},{4,6},{6,4},{5,7},{7,5},{8,10},{10,8},{9,1... | collective-permute-start | bytes 3145736 | tf_op jit(solution)/shard_map/ppermute | solution.py:51
  138.8 14.9 %collective-permute-start.19 = (bf16[64,2560]{1,0:T(8,128)(2,1)S(1)}, bf16[64,2560]{1,0:T(8,128)(2,1)S(1)}, u32[]{:S(2)}, u32[]{:S(2)}) collective-permute-start(bf16[64,2560]{1,0:T(8,128)(2,1)S(1)} %slice.246), channel_id=1, source_target_pairs={{0,96},{32,0},{64,32},{96,64},{1,97},{33,1},{65,33},{97,65},{2,98}... | collective-permute-start | bytes 983048 | tf_op jit(solution)/shard_map/ppermute | solution.py:43
  151.4 30.4 %collective-permute-start.15 = (bf16[128,2560]{1,0:T(8,128)(2,1)S(1)}, bf16[128,2560]{1,0:T(8,128)(2,1)S(1)}, u32[]{:S(2)}, u32[]{:S(2)}) collective-permute-start(bf16[128,2560]{1,0:T(8,128)(2,1)S(1)} %fusion.7), channel_id=1, source_target_pairs={{0,1},{1,0},{2,3},{3,2},{4,5},{5,4},{6,7},{7,6},{8,9},{9,8},{10,11... | collective-permute-start | bytes 1966088 | tf_op jit(solution)/shard_map/ppermute | solution.py:47
  183.4 15.2 %collective-permute-start.21 = (bf16[128,2560]{1,0:T(8,128)(2,1)S(1)}, bf16[128,2560]{1,0:T(8,128)(2,1)S(1)}, u32[]{:S(2)}, u32[]{:S(2)}) collective-permute-start(bf16[128,2560]{1,0:T(8,128)(2,1)S(1)} %get-tuple-element.117), channel_id=1, source_target_pairs={{0,32},{32,64},{64,96},{96,0},{1,33},{33,65},{65,97},{97,1},{2,34}... | collective-permute-start | bytes 1966088 | tf_op jit(solution)/shard_map/ppermute | solution.py:43
  187.0 15.4 %collective-permute-start.20 = (bf16[128,2560]{1,0:T(8,128)(2,1)S(1)}, bf16[128,2560]{1,0:T(8,128)(2,1)S(1)}, u32[]{:S(2)}, u32[]{:S(2)}) collective-permute-start(bf16[128,2560]{1,0:T(8,128)(2,1)S(1)} %get-tuple-element.117), channel_id=1, source_target_pairs={{0,96},{32,0},{64,32},{96,64},{1,97},{33,1},{65,33},{97,65},{2,98}... | collective-permute-start | bytes 1966088 | tf_op jit(solution)/shard_map/ppermute | solution.py:43
  202.4 8.8 %collective-permute-start.23 = (bf16[64,2560]{1,0:T(8,128)(2,1)S(1)}, bf16[64,2560]{1,0:T(8,128)(2,1)S(1)}, u32[]{:S(2)}, u32[]{:S(2)}) collective-permute-start(bf16[64,2560]{1,0:T(8,128)(2,1)S(1)} %slice.248), channel_id=1, source_target_pairs={{0,96},{32,0},{64,32},{96,64},{1,97},{33,1},{65,33},{97,65},{2,98}... | collective-permute-start | bytes 983048 | tf_op jit(solution)/shard_map/ppermute | solution.py:43
  248.8 11.1 %collective-permute-start.24 = (bf16[64,2560]{1,0:T(8,128)(2,1)S(1)}, bf16[64,2560]{1,0:T(8,128)(2,1)S(1)}, u32[]{:S(2)}, u32[]{:S(2)}) collective-permute-start(bf16[64,2560]{1,0:T(8,128)(2,1)S(1)} %get-tuple-element.156), channel_id=1, source_target_pairs={{0,96},{32,0},{64,32},{96,64},{1,97},{33,1},{65,33},{97,65},{2,98}... | collective-permute-start | bytes 983048 | tf_op jit(solution)/shard_map/ppermute | solution.py:43
  249.2 11.0 %collective-permute-start.26 = (bf16[64,2560]{1,0:T(8,128)(2,1)S(1)}, bf16[64,2560]{1,0:T(8,128)(2,1)S(1)}, u32[]{:S(2)}, u32[]{:S(2)}) collective-permute-start(bf16[64,2560]{1,0:T(8,128)(2,1)S(1)} %get-tuple-element.157), channel_id=1, source_target_pairs={{0,32},{32,64},{64,96},{96,0},{1,33},{33,65},{65,97},{97,1},{2,34}... | collective-permute-start | bytes 983048 | tf_op jit(solution)/shard_map/ppermute | solution.py:43
  260.1 11.9 %collective-permute-start.25 = (bf16[128,2560]{1,0:T(8,128)(2,1)S(1)}, bf16[128,2560]{1,0:T(8,128)(2,1)S(1)}, u32[]{:S(2)}, u32[]{:S(2)}) collective-permute-start(bf16[128,2560]{1,0:T(8,128)(2,1)S(1)} %fusion.18), channel_id=1, source_target_pairs={{0,96},{32,0},{64,32},{96,64},{1,97},{33,1},{65,33},{97,65},{2,98}... | collective-permute-start | bytes 1966088 | tf_op jit(solution)/shard_map/ppermute | solution.py:43
  260.4 11.6 %collective-permute-start.27 = (bf16[128,2560]{1,0:T(8,128)(2,1)S(1)}, bf16[128,2560]{1,0:T(8,128)(2,1)S(1)}, u32[]{:S(2)}, u32[]{:S(2)}) collective-permute-start(bf16[128,2560]{1,0:T(8,128)(2,1)S(1)} %fusion.19), channel_id=1, source_target_pairs={{0,32},{32,64},{64,96},{96,0},{1,33},{33,65},{65,97},{97,1},{2,34}... | collective-permute-start | bytes 1966088 | tf_op jit(solution)/shard_map/ppermute | solution.py:43
  272.2 19.8 %collective-permute-start.28 = (bf16[128,2560]{1,0:T(8,128)(2,1)S(1)}, bf16[128,2560]{1,0:T(8,128)(2,1)}, u32[]{:S(2)}, u32[]{:S(2)}) collective-permute-start(bf16[128,2560]{1,0:T(8,128)(2,1)S(1)} %reduce-precision_convert_fusion.1), channel_id=1, source_target_pairs={{0,1},{1,0},{2,3},{3,2},{4,5},{5,4},{6,7},{7,6},{8,9},{9,8},{10,11... | collective-permute-start | bytes 1966088 | tf_op jit(solution)/shard_map/ppermute | solution.py:47
  312.4 18.3 %collective-permute-start.29 = (bf16[128,2560]{1,0:T(8,128)(2,1)}, bf16[128,2560]{1,0:T(8,128)(2,1)S(1)}, u32[]{:S(2)}, u32[]{:S(2)}) collective-permute-start(bf16[128,2560]{1,0:T(8,128)(2,1)} %get-tuple-element.66.refs_5_.refs_0_), channel_id=1, source_target_pairs={{0,96},{32,0},{64,32},{96,64},{1,97},{33,1},{65,33},{97,65},{2,98}... | collective-permute-start | bytes 1966088 | tf_op jit(solution)/shard_map/ppermute | solution.py:43
  312.4 20.5 %collective-permute-start.30 = (bf16[128,2560]{1,0:T(8,128)(2,1)}, bf16[128,2560]{1,0:T(8,128)(2,1)S(1)}, u32[]{:S(2)}, u32[]{:S(2)}) collective-permute-start(bf16[128,2560]{1,0:T(8,128)(2,1)} %get-tuple-element.66.refs_5_.refs_0_), channel_id=1, source_target_pairs={{0,64},{32,96},{64,0},{96,32},{1,65},{33,97},{65,1},{97,33},{2,66}... | collective-permute-start | bytes 1966088 | tf_op jit(solution)/shard_map/ppermute | solution.py:43
  317.1 15.8 %collective-permute-start.31 = (bf16[128,2560]{1,0:T(8,128)(2,1)}, bf16[128,2560]{1,0:T(8,128)(2,1)S(1)}, u32[]{:S(2)}, u32[]{:S(2)}) collective-permute-start(bf16[128,2560]{1,0:T(8,128)(2,1)} %get-tuple-element.66.refs_5_.refs_0_), channel_id=1, source_target_pairs={{0,32},{32,64},{64,96},{96,0},{1,33},{33,65},{65,97},{97,1},{2,34}... | collective-permute-start | bytes 1966088 | tf_op jit(solution)/shard_map/ppermute | solution.py:43
  317.1 55.9 %collective-permute-start.42 = (f32[1,128]{1,0:T(1,128)S(1)}, f32[1,128]{1,0:T(1,128)S(1)}, u32[]{:S(2)}, u32[]{:S(2)}) collective-permute-start(f32[1,128]{1,0:T(1,128)S(1)} %bitcast.206), channel_id=1, source_target_pairs={{0,32},{32,64},{64,96},{96,0},{1,33},{33,65},{65,97},{97,1},{2,34}... | collective-permute-start | bytes 1544 | tf_op jit(solution)/shard_map/ppermute | solution.py:43
  322.9 47.5 %all-to-all-start.4 = ((bf16[32,128,256]{2,1,0:T(8,128)(2,1)}), bf16[32,128,256]{2,1,0:T(8,128)(2,1)}, u32[]{:S(2)}, u32[]{:S(2)}) async-start(bf16[32,128,256]{2,1,0:T(8,128)(2,1)} %bitcast.183), calls=%async_computation.5 | async-start | bytes 4194304 | tf_op jit(solution)/shard_map/all_to_all | solution.py:684
  334.3 9.3 %collective-permute-start.33 = (bf16[640,128]{1,0:T(8,128)(2,1)S(1)}, bf16[640,128]{1,0:T(8,128)(2,1)S(1)}, u32[]{:S(2)}, u32[]{:S(2)}) collective-permute-start(bf16[640,128]{1,0:T(8,128)(2,1)S(1)} %get-tuple-element.153), channel_id=1, source_target_pairs={{0,64},{32,96},{64,0},{96,32},{1,65},{33,97},{65,1},{97,33},{2,66}... | collective-permute-start | bytes 491528 | tf_op jit(solution)/shard_map/ppermute | solution.py:43
  338.3 34.7 %collective-permute-start.41 = (bf16[128,256]{1,0:T(8,128)(2,1)S(1)}, bf16[128,256]{1,0:T(8,128)(2,1)S(1)}, u32[]{:S(2)}, u32[]{:S(2)}) collective-permute-start(bf16[128,256]{1,0:T(8,128)(2,1)S(1)} %select_bitcast_fusion), channel_id=1, source_target_pairs={{0,1},{1,0},{2,3},{3,2},{4,5},{5,4},{6,7},{7,6},{8,9},{9,8},{10,11... | collective-permute-start | bytes 196616 | tf_op jit(solution)/shard_map/ppermute | solution.py:47
  348.8 10.3 %collective-permute-start.35 = (bf16[64,2560]{1,0:T(8,128)(2,1)S(1)}, bf16[64,2560]{1,0:T(8,128)(2,1)S(1)}, u32[]{:S(2)}, u32[]{:S(2)}) collective-permute-start(bf16[64,2560]{1,0:T(8,128)(2,1)S(1)} %get-tuple-element.150), channel_id=1, source_target_pairs={{0,96},{32,0},{64,32},{96,64},{1,97},{33,1},{65,33},{97,65},{2,98}... | collective-permute-start | bytes 983048 | tf_op jit(solution)/shard_map/ppermute | solution.py:43
  350.6 8.8 %collective-permute-start.37 = (bf16[64,2560]{1,0:T(8,128)(2,1)S(1)}, bf16[64,2560]{1,0:T(8,128)(2,1)S(1)}, u32[]{:S(2)}, u32[]{:S(2)}) collective-permute-start(bf16[64,2560]{1,0:T(8,128)(2,1)S(1)} %get-tuple-element.151), channel_id=1, source_target_pairs={{0,32},{32,64},{64,96},{96,0},{1,33},{33,65},{65,97},{97,1},{2,34}... | collective-permute-start | bytes 983048 | tf_op jit(solution)/shard_map/ppermute | solution.py:43
  358.3 16.9 %collective-permute-start.39 = (bf16[8,40,2560]{2,1,0:T(8,128)(2,1)}, bf16[8,40,2560]{2,1,0:T(8,128)(2,1)}, u32[]{:S(2)}, u32[]{:S(2)}) collective-permute-start(bf16[8,40,2560]{2,1,0:T(8,128)(2,1)} %dynamic-slice_bitcast_fusion), channel_id=1, source_target_pairs={{0,2},{2,0},{1,3},{3,1},{4,6},{6,4},{5,7},{7,5},{8,10},{10,8},{9,1... | collective-permute-start | bytes 4915208 | tf_op jit(solution)/shard_map/ppermute | solution.py:51
  360.6 34.5 %collective-permute-start.36 = (bf16[128,2560]{1,0:T(8,128)(2,1)}, bf16[128,2560]{1,0:T(8,128)(2,1)}, u32[]{:S(2)}, u32[]{:S(2)}) collective-permute-start(bf16[128,2560]{1,0:T(8,128)(2,1)} %fusion.20), channel_id=1, source_target_pairs={{0,96},{32,0},{64,32},{96,64},{1,97},{33,1},{65,33},{97,65},{2,98}... | collective-permute-start | bytes 1966088 | tf_op jit(solution)/shard_map/ppermute | solution.py:43
  363.2 31.9 %collective-permute-start.38 = (bf16[128,2560]{1,0:T(8,128)(2,1)}, bf16[128,2560]{1,0:T(8,128)(2,1)}, u32[]{:S(2)}, u32[]{:S(2)}) collective-permute-start(bf16[128,2560]{1,0:T(8,128)(2,1)} %fusion.21), channel_id=1, source_target_pairs={{0,32},{32,64},{64,96},{96,0},{1,33},{33,65},{65,97},{97,1},{2,34}... | collective-permute-start | bytes 1966088 | tf_op jit(solution)/shard_map/ppermute | solution.py:43
  373.1 12.7 %collective-permute-start.43 = (bf16[256,256]{1,0:T(8,128)(2,1)S(1)}, bf16[256,256]{1,0:T(8,128)(2,1)S(1)}, u32[]{:S(2)}, u32[]{:S(2)}) collective-permute-start(bf16[256,256]{1,0:T(8,128)(2,1)S(1)} %fusion.29.refs_4_), channel_id=1, source_target_pairs={{0,96},{32,0},{64,32},{96,64},{1,97},{33,1},{65,33},{97,65},{2,98}... | collective-permute-start | bytes 393224 | tf_op jit(solution)/shard_map/ppermute | solution.py:43
  374.0 11.8 %collective-permute-start.44 = (bf16[256,256]{1,0:T(8,128)(2,1)S(1)}, bf16[256,256]{1,0:T(8,128)(2,1)}, u32[]{:S(2)}, u32[]{:S(2)}) collective-permute-start(bf16[256,256]{1,0:T(8,128)(2,1)S(1)} %fusion.29.refs_4_), channel_id=1, source_target_pairs={{0,64},{32,96},{64,0},{96,32},{1,65},{33,97},{65,1},{97,33},{2,66}... | collective-permute-start | bytes 393224 | tf_op jit(solution)/shard_map/ppermute | solution.py:43
  375.2 10.7 %collective-permute-start.45 = (bf16[256,256]{1,0:T(8,128)(2,1)S(1)}, bf16[256,256]{1,0:T(8,128)(2,1)}, u32[]{:S(2)}, u32[]{:S(2)}) collective-permute-start(bf16[256,256]{1,0:T(8,128)(2,1)S(1)} %fusion.29.refs_4_), channel_id=1, source_target_pairs={{0,32},{32,64},{64,96},{96,0},{1,33},{33,65},{65,97},{97,1},{2,34}... | collective-permute-start | bytes 393224 | tf_op jit(solution)/shard_map/ppermute | solution.py:43
  380.3 25.6 %all-to-all-start.3 = ((bf16[8,40,2560]{2,1,0:T(8,128)(2,1)}), bf16[8,40,2560]{2,1,0:T(8,128)(2,1)}, u32[]{:S(2)}, u32[]{:S(2)}) async-start(bf16[8,40,2560]{2,1,0:T(8,128)(2,1)} %fusion.9), calls=%async_computation.4 | async-start | bytes 3276800 | tf_op jit(solution)/shard_map/all_to_all | solution.py:706
  405.9 40.1 %collective-permute-start.49 = (bf16[128,2560]{0,1:T(8,128)(2,1)S(1)}, bf16[128,2560]{0,1:T(8,128)(2,1)}, u32[]{:S(2)}, u32[]{:S(2)}) collective-permute-start(bf16[128,2560]{0,1:T(8,128)(2,1)S(1)} %reduce-precision_convert_fusion), channel_id=1, source_target_pairs={{0,1},{1,0},{2,3},{3,2},{4,5},{5,4},{6,7},{7,6},{8,9},{9,8},{10,11... | collective-permute-start | bytes 1966088 | tf_op jit(solution)/shard_map/ppermute | solution.py:47
  408.7 17.4 %collective-permute-start.50 = (bf16[40,3072]{1,0:T(8,128)(2,1)}, bf16[40,3072]{1,0:T(8,128)(2,1)}, u32[]{:S(2)}, u32[]{:S(2)}) collective-permute-start(bf16[40,3072]{1,0:T(8,128)(2,1)} %get-tuple-element.145), channel_id=1, source_target_pairs={{0,32},{32,64},{64,96},{96,0},{1,33},{33,65},{65,97},{97,1},{2,34}... | collective-permute-start | bytes 737288 | tf_op jit(solution)/shard_map/ppermute | solution.py:43
  409.6 16.5 %collective-permute-start.51 = (bf16[40,3072]{1,0:T(8,128)(2,1)}, bf16[40,3072]{1,0:T(8,128)(2,1)}, u32[]{:S(2)}, u32[]{:S(2)}) collective-permute-start(bf16[40,3072]{1,0:T(8,128)(2,1)} %get-tuple-element.144), channel_id=1, source_target_pairs={{0,64},{32,96},{64,0},{96,32},{1,65},{33,97},{65,1},{97,33},{2,66}... | collective-permute-start | bytes 737288 | tf_op jit(solution)/shard_map/ppermute | solution.py:43
  411.0 15.1 %collective-permute-start.52 = (bf16[40,3072]{1,0:T(8,128)(2,1)}, bf16[40,3072]{1,0:T(8,128)(2,1)}, u32[]{:S(2)}, u32[]{:S(2)}) collective-permute-start(bf16[40,3072]{1,0:T(8,128)(2,1)} %get-tuple-element.143), channel_id=1, source_target_pairs={{0,96},{32,0},{64,32},{96,64},{1,97},{33,1},{65,33},{97,65},{2,98}... | collective-permute-start | bytes 737288 | tf_op jit(solution)/shard_map/ppermute | solution.py:43
  413.4 30.2 %collective-permute-start.40 = (bf16[128,2560]{0,1:T(8,128)(2,1)}, bf16[128,2560]{0,1:T(8,128)(2,1)}, u32[]{:S(2)}, u32[]{:S(2)}) collective-permute-start(bf16[128,2560]{0,1:T(8,128)(2,1)} %bitcast.55), channel_id=1, source_target_pairs={{0,1},{1,0},{2,3},{3,2},{4,5},{5,4},{6,7},{7,6},{8,9},{9,8},{10,11... | collective-permute-start | bytes 1966088 | tf_op jit(solution)/shard_map/ppermute | solution.py:47
  418.7 23.9 %all-to-all-start.5 = ((bf16[16,40,256]{2,1,0:T(8,128)(2,1)}), bf16[16,40,256]{2,1,0:T(8,128)(2,1)}, u32[]{:S(2)}, u32[]{:S(2)}) async-start(bf16[16,40,256]{2,1,0:T(8,128)(2,1)} %bitcast.87), calls=%async_computation.6 | async-start | bytes 655360 | tf_op jit(solution)/shard_map/all_to_all | solution.py:719
  445.9 12.1 %collective-permute-start.53 = (f32[2,40]{1,0:T(2,128)S(1)}, f32[2,40]{1,0:T(2,128)S(1)}, u32[]{:S(2)}, u32[]{:S(2)}) collective-permute-start(f32[2,40]{1,0:T(2,128)S(1)} %pad_maximum_fusion.6), channel_id=1, source_target_pairs={{0,1},{1,0},{2,3},{3,2},{4,5},{5,4},{6,7},{7,6},{8,9},{9,8},{10,11... | collective-permute-start | bytes 968 | tf_op jit(solution)/shard_map/ppermute | solution.py:47
  447.6 10.9 %collective-permute-start.54 = (f32[40,256]{1,0:T(8,128)S(1)}, f32[40,256]{1,0:T(8,128)S(1)}, u32[]{:S(2)}, u32[]{:S(2)}) collective-permute-start(f32[40,256]{1,0:T(8,128)S(1)} %convert_reduce_fusion.3), channel_id=1, source_target_pairs={{0,1},{1,0},{2,3},{3,2},{4,5},{5,4},{6,7},{7,6},{8,9},{9,8},{10,11... | collective-permute-start | bytes 122888 | tf_op jit(solution)/shard_map/ppermute | solution.py:47
  (82 other events, 839.4 us)
Sparse Core Ops, SparseCore 0:
  23.3 56.6 all-gather.2
  81.6 112.1 all-gather.4
  238.7 127.5 reduce-scatter.1
